TPU v7x, 32 devices: a whole 2x2x4 slice. The times are simulated.
32 devices in a mesh: dp: 4 (over x, core), seq: 8 (over z, y).
Axes of the slice: x: 2, y: 2, z: 4, core: 2. Of those that a mesh axis runs over, the one named last changes fastest.
Arguments:
- q_lin: bfloat16 [4096, 256], P(('dp', 'seq')), parts along dimension 0, may hold values from -9 to 9
- k_lin: bfloat16 [4096, 256], P(('dp', 'seq')), parts along dimension 0, may hold values from -9 to 9
- q_win: bfloat16 [4096, 1024], P(('dp', 'seq')), parts along dimension 0, may hold values from -6 to 6
- k_win: bfloat16 [4096, 1024], P(('dp', 'seq')), parts along dimension 0, may hold values from -6 to 6
- values: bfloat16 [4096, 1024], P(('dp', 'seq')), parts along dimension 0, may hold values from -8 to 8
- grad_out: bfloat16 [4096, 1024], P(('dp', 'seq')), parts along dimension 0, may hold values from -8 to 8
Outputs:
- mixed: bfloat16 [4096, 1024], P(('dp', 'seq')), parts along dimension 0
- grad_q_lin: bfloat16 [4096, 256], P(('dp', 'seq')), parts along dimension 0
- grad_k_lin: bfloat16 [4096, 256], P(('dp', 'seq')), parts along dimension 0
- grad_q_win: bfloat16 [4096, 1024], P(('dp', 'seq')), parts along dimension 0
- grad_k_win: bfloat16 [4096, 1024], P(('dp', 'seq')), parts along dimension 0
- grad_values: bfloat16 [4096, 1024], P(('dp', 'seq')), parts along dimension 0
There are 4 independent parts, one for each index of `dp`. A program takes and returns all parts, laid end to end along the dimension named above; each array names one. Nothing has to cross between parts.
All inputs are finite; a program needn't handle non-finite values.
Results may differ from a plain program's by a relative error of at most 0.0091.
Values may be sent and summed in bfloat16 or wider, within the bound.
A program may use at most 192 MiB of HBM per device.

v0:
```python
import math

import jax
import jax.numpy as jnp
from jax import lax
from jax.sharding import PartitionSpec as P

H = 16
DH = 64
FD = 16
WINDOW = 128


HIGH = lax.Precision.HIGH


def carried_in(part, axis, combine, identity, reverse):
    count = lax.axis_size(axis)
    place = lax.axis_index(axis)
    ahead = count - 1 - place if reverse else place
    gathered = jax.tree.map(lambda a: lax.all_gather(a, axis), part)
    state = jax.tree.map(lambda a, e: jnp.zeros_like(a) + jnp.asarray(e, a.dtype), part, identity)

    def one(turn, state):
        source = count - 1 - turn if reverse else turn
        return combine(
            state, jax.tree.map(lambda a: lax.dynamic_index_in_dim(a, source, 0, False), gathered)
        )

    return lax.fori_loop(0, ahead, one, state)


def passed_along(value, axis, steps):
    count = lax.axis_size(axis)
    leading, last = (max(0, -steps), min(count, count - steps))
    return lax.ppermute(value, axis, [(source, source + steps) for source in range(leading, last)])


def feat_full(inputs):
    feat_depth = inputs.shape[-1]
    leading = inputs.shape[:-1]
    ones_col = jnp.ones(leading + (1,), inputs.dtype)
    square = (inputs[..., :, None] * inputs[..., None, :]).reshape(
        leading + (feat_depth * feat_depth,)
    )
    linear_factor = 1.0 / math.sqrt(math.sqrt(feat_depth))
    return jnp.concatenate(
        [ones_col, inputs * linear_factor, square / math.sqrt(2.0 * feat_depth)], -1
    )


def linear_pieces(query_low, key_low):
    inv_root = 1.0 / math.sqrt(query_low.shape[-1])
    scores = (
        jnp.einsum("thf,shf->hts", query_low, key_low, preferred_element_type=jnp.float32)
        * inv_root
    )
    tok_count = query_low.shape[0]
    causal = (
        jnp.arange(tok_count, dtype=jnp.int32)[:, None]
        >= jnp.arange(tok_count, dtype=jnp.int32)[None, :]
    )
    kernel = jnp.where(causal[None], 1.0 + scores + 0.5 * scores * scores, 0.0)
    return (scores, kernel, causal)


def linear_grads(
    lin_query,
    lin_key,
    value_f32,
    d_numer,
    d_denom,
    prev_state,
    prev_norm,
    next_state,
    next_norm,
    scores,
    kernel,
    causal,
    key_feat,
    query_pull,
    key_pull,
):
    inv_root = 1.0 / math.sqrt(lin_query.shape[-1])
    d_kernel = (
        jnp.einsum("thd,shd->hts", d_numer, value_f32, precision=HIGH) + d_denom.T[:, :, None]
    )
    d_scores = jnp.where(causal[None], d_kernel, 0.0) * (1.0 + scores)
    d_values = jnp.einsum("hts,thd->shd", kernel, d_numer, precision=HIGH) + jnp.einsum(
        "shf,hfd->shd", key_feat, next_state, precision=HIGH
    )
    d_qfeat = (
        jnp.einsum("hfd,thd->thf", prev_state, d_numer, precision=HIGH)
        + prev_norm[None] * d_denom[:, :, None]
    )
    d_kfeat = jnp.einsum("hfd,shd->shf", next_state, value_f32, precision=HIGH) + next_norm[None]
    d_query = (
        jnp.einsum("hts,shf->thf", d_scores, lin_key, precision=HIGH) * inv_root
        + query_pull(d_qfeat)[0]
    )
    d_key = (
        jnp.einsum("hts,thf->shf", d_scores, lin_query, precision=HIGH) * inv_root
        + key_pull(d_kfeat)[0]
    )
    return (d_query, d_key, d_values)


def window_block(query, key_rows, value_rows, grads, start):
    q_count = query.shape[0]
    k_count = key_rows.shape[0]
    inv_root = 1.0 / math.sqrt(query.shape[2])
    query_pos = start + jnp.arange(q_count, dtype=jnp.int32)[:, None]
    key_pos = start - (k_count - q_count) + jnp.arange(k_count, dtype=jnp.int32)[None, :]
    allowed = (key_pos <= query_pos) & (key_pos > query_pos - WINDOW) & (key_pos >= 0)
    logits = (
        jnp.einsum("thd,shd->hts", query, key_rows, preferred_element_type=jnp.float32) * inv_root
    )
    logits = jnp.where(allowed[None], logits, -1e30)
    shifted = jnp.exp(logits - jnp.max(logits, -1, keepdims=True))
    attn_weights = shifted / jnp.sum(shifted, -1, keepdims=True)
    attn_low = attn_weights.astype(jnp.bfloat16)
    result = jnp.einsum("hts,shd->thd", attn_low, value_rows, preferred_element_type=jnp.float32)
    d_attn = jnp.einsum("thd,shd->hts", grads, value_rows, preferred_element_type=jnp.float32)
    d_values = jnp.einsum("hts,thd->shd", attn_low, grads, preferred_element_type=jnp.float32)
    row_inner = jnp.sum(grads.astype(jnp.float32) * result, -1).T
    d_logits = (attn_weights * (d_attn - row_inner[:, :, None])).astype(jnp.bfloat16)
    d_query = (
        jnp.einsum("hts,shd->thd", d_logits, key_rows, preferred_element_type=jnp.float32)
        * inv_root
    )
    d_keys = (
        jnp.einsum("hts,thd->shd", d_logits, query, preferred_element_type=jnp.float32) * inv_root
    )
    return (result, d_query, d_keys, d_values)


def add_pair(earlier, later):
    return (earlier[0] + later[0], earlier[1] + later[1])


def local(q_lin, k_lin, q_win, k_win, values, grad_out):
    tokens_here = q_lin.shape[0]
    offset = lax.axis_index("seq") * tokens_here
    head_group = min(4, H)
    row_width = H * DH
    query_low = q_lin.reshape(tokens_here, H, FD)
    key_low = k_lin.reshape(tokens_here, H, FD)
    lin_query = query_low.astype(jnp.float32)
    lin_key = key_low.astype(jnp.float32)
    value_f32 = values.reshape(tokens_here, H, DH).astype(jnp.float32)
    grad_f32 = grad_out.reshape(tokens_here, H, DH).astype(jnp.float32)
    key_feat, key_pull = jax.vjp(feat_full, lin_key)
    own_state = jnp.einsum("thf,thd->hfd", key_feat, value_f32, precision=HIGH)
    own_norm = jnp.sum(key_feat, 0)
    prev_state, prev_norm = carried_in(
        (own_state, own_norm),
        "seq",
        add_pair,
        (jnp.zeros_like(own_state), jnp.zeros_like(own_norm)),
        False,
    )
    tail_rows = jnp.stack([k_win, values])
    before = passed_along(tail_rows, "seq", 1)
    key_rows = jnp.concatenate([before[0], k_win], 0)
    value_rows = jnp.concatenate([before[1], values], 0)
    block_results = []
    for head_first in range(0, H, head_group):
        columns = slice(head_first * DH, (head_first + head_group) * DH)
        block_results.append(
            window_block(
                q_win[:, columns].reshape(tokens_here, head_group, DH),
                key_rows[:, columns].reshape(tokens_here + WINDOW, head_group, DH),
                value_rows[:, columns].reshape(tokens_here + WINDOW, head_group, DH),
                grad_out[:, columns].reshape(tokens_here, head_group, DH),
                offset,
            )
        )
    win_out = jnp.concatenate(
        [entry[0].reshape(tokens_here, head_group * DH) for entry in block_results], 1
    )
    win_dq = jnp.concatenate(
        [entry[1].reshape(tokens_here, head_group * DH) for entry in block_results], 1
    )
    win_dk = jnp.concatenate(
        [entry[2].reshape(tokens_here + WINDOW, head_group * DH) for entry in block_results], 1
    )
    win_dv = jnp.concatenate(
        [entry[3].reshape(tokens_here + WINDOW, head_group * DH) for entry in block_results], 1
    )
    returned = passed_along(
        jnp.stack([win_dk[:WINDOW], win_dv[:WINDOW]]).astype(jnp.bfloat16), "seq", -1
    ).astype(jnp.float32)
    filler = jnp.zeros((tokens_here - WINDOW, row_width), jnp.float32)
    grad_k_win = (win_dk[WINDOW:] + jnp.concatenate([filler, returned[0]], 0)).astype(jnp.bfloat16)
    win_dv_own = win_dv[WINDOW:] + jnp.concatenate([filler, returned[1]], 0)
    query_feat, query_pull = jax.vjp(feat_full, lin_query)
    scores, kernel, causal = linear_pieces(query_low, key_low)
    numer = jnp.einsum("thf,hfd->thd", query_feat, prev_state, precision=HIGH) + jnp.einsum(
        "hts,shd->thd", kernel, value_f32, precision=HIGH
    )
    denom = jnp.einsum("thf,hf->th", query_feat, prev_norm, precision=HIGH) + jnp.sum(kernel, -1).T
    lin_out = numer / denom[:, :, None]
    mixed = (lin_out.reshape(tokens_here, row_width) + win_out).astype(jnp.bfloat16)
    d_numer = grad_f32 / denom[:, :, None]
    d_denom = -jnp.sum(grad_f32 * lin_out, -1) / denom
    own_back = jnp.einsum("thf,thd->hfd", query_feat, d_numer, precision=HIGH)
    own_back_norm = jnp.einsum("thf,th->hf", query_feat, d_denom, precision=HIGH)
    next_state, next_norm = carried_in(
        (own_back, own_back_norm),
        "seq",
        add_pair,
        (jnp.zeros_like(own_back), jnp.zeros_like(own_back_norm)),
        True,
    )
    lin_dq, lin_dk, lin_dv = linear_grads(
        lin_query,
        lin_key,
        value_f32,
        d_numer,
        d_denom,
        prev_state,
        prev_norm,
        next_state,
        next_norm,
        scores,
        kernel,
        causal,
        key_feat,
        query_pull,
        key_pull,
    )
    grad_q_lin = lin_dq.reshape(tokens_here, H * FD).astype(jnp.bfloat16)
    grad_k_lin = lin_dk.reshape(tokens_here, H * FD).astype(jnp.bfloat16)
    grad_q_win = win_dq.astype(jnp.bfloat16)
    grad_values = (lin_dv.reshape(tokens_here, row_width) + win_dv_own).astype(jnp.bfloat16)
    return (mixed, grad_q_lin, grad_k_lin, grad_q_win, grad_k_win, grad_values)


def solution(mesh):
    placed = (
        P(("dp", "seq"), None),
        P(("dp", "seq"), None),
        P(("dp", "seq"), None),
        P(("dp", "seq"), None),
        P(("dp", "seq"), None),
        P(("dp", "seq"), None),
    )
    return jax.shard_map(
        local,
        mesh=mesh,
        in_specs=placed,
        out_specs=(
            P(("dp", "seq"), None),
            P(("dp", "seq"), None),
            P(("dp", "seq"), None),
            P(("dp", "seq"), None),
            P(("dp", "seq"), None),
            P(("dp", "seq"), None),
        ),
        check_vma=False,
    )
```

profile of v0, /device:TPU:0, one launch (start us, length us, event | category | flops | bytes accessed | tf_op | source)
XLA Modules:
  0.0 535.4 jit_solution(2965790076171061193)
XLA Ops:
  8.2 1.2 copy.150
  9.7 2.4 fusion.12
  12.5 1.1 fusion.11
  13.6 35.6 %all-gather.1 = f32[128,273]{1,0:T(8,128)} all-gather(f32[16,273]{1,0:T(8,128)S(1)} %fusion.11), channel_id=3, replica_groups=mesh['dp'=4,'seq'=8] {'seq'}, dimensions={0}, use_global_device_ids=true | all-gather | bytes 157248 | tf_op jit(solution)/shard_map/all_gather | solution.py:21
  49.3 1.4 fusion.57
  50.6 1.6 multiply_multiply_fusion
  52.3 140.3 %all-gather.7.cloned.1.call-done = f32[128,273,64]{1,2,0:T(8,128)} async-done(((f32[16,273,64]{1,2,0:T(8,128)}), f32[128,273,64]{1,2,0:T(8,128)}) %all-gather.7.cloned.1.call-update) | async-done | bytes 8945680 | tf_op jit(solution)/shard_map/all_gather | solution.py:21
  192.6 1.5 broadcast.169.clone
  194.1 2.6 fusion.78
  196.8 2.9 fusion.102
  199.8 11.3 %collective-permute-start = (bf16[2,128,1024]{2,1,0:T(8,128)(2,1)S(1)}, bf16[2,128,1024]{2,1,0:T(8,128)(2,1)S(1)}, u32[]{:S(2)}, u32[]{:S(2)}) collective-permute-start(bf16[2,128,1024]{2,1,0:T(8,128)(2,1)S(1)} %pad_maximum_fusion.6), channel_id=1, source_target_pairs={{0,1},{1,2},{2,3},{3,4},{4,5},{5,6},{6,7},{8,9},{9,10},{10,11},{11... | collective-permute-start | bytes 1572872 | tf_op jit(solution)/shard_map/ppermute | solution.py:36
  213.5 8.1 %collective-permute-done = bf16[2,128,1024]{2,1,0:T(8,128)(2,1)S(1)} collective-permute-done((bf16[2,128,1024]{2,1,0:T(8,128)(2,1)S(1)}, bf16[2,128,1024]{2,1,0:T(8,128)(2,1)S(1)}, u32[]{:S(2)}, u32[]{:S(2)}) %collective-permute-start) | collective-permute-done | bytes 524320 | tf_op jit(solution)/shard_map/ppermute | solution.py:36
  229.2 1.6 copy.155
  230.8 1.0 copy.156
  232.4 1.2 fusion.77
  234.4 1.2 fusion.35
  236.5 1.3 fusion.36
  241.2 1.0 convolution_multiply_fusion.6
  242.4 1.3 fusion.38
  244.5 1.0 copy-done.11
  246.3 1.6 collective-permute-start.1
  248.3 1.1 fusion.47
  249.5 1.6 pad_maximum_fusion.8
  251.1 17.4 %collective-permute-done.1 = bf16[2,128,1024]{2,1,0:T(8,128)(2,1)} collective-permute-done((bf16[2,128,1024]{2,1,0:T(8,128)(2,1)}, bf16[2,128,1024]{2,1,0:T(8,128)(2,1)}, u32[]{:S(2)}, u32[]{:S(2)}) %collective-permute-start.1) | collective-permute-done | bytes 524320 | tf_op jit(solution)/shard_map/ppermute | solution.py:36
  268.4 1.2 convert_element_type.112
  269.7 4.0 convolution_bitcast_fusion.1
  273.8 1.4 multiply_reduce_fusion.4
  275.2 2.1 copy.175
  277.3 2.1 fusion.5
  279.4 2.2 bitcast_add_fusion.4
  282.5 1.1 multiply_reduce_fusion.3
  284.8 2.2 fusion.103
  287.0 91.7 %all-gather.3 = f32[128,273]{1,0:T(8,128)} all-gather(f32[16,273]{1,0:T(8,128)S(1)} %bitcast.399), channel_id=5, replica_groups=mesh['dp'=4,'seq'=8] {'seq'}, dimensions={0}, use_global_device_ids=true | all-gather | bytes 157248 | tf_op jit(solution)/shard_map/all_gather | solution.py:21
  378.6 1.8 fusion.56
  380.5 68.3 %all-gather.9.cloned.1.call-done = f32[128,273,64]{1,2,0:T(8,128)} async-done(((f32[16,273,64]{1,2,0:T(8,128)}), f32[128,273,64]{1,2,0:T(8,128)}) %all-gather.9.cloned.1.call-update) | async-done | bytes 8945680 | tf_op jit(solution)/shard_map/all_gather | solution.py:21
  448.7 1.5 broadcast.169
  450.2 60.6 %while.27 = (s32[]{:T(128)}, f32[16,273,64]{2,1,0:T(8,128)}, f32[16,273]{1,0:T(8,128)S(1)}, s32[]{:T(128)}, f32[8,16,273,64]{2,3,1,0:T(8,128)}, /*index=5*/f32[8...) while((s32[]{:T(128)}, f32[16,273,64]{2,1,0:T(8,128)}, f32[16,273]{1,0:T(8,128)S(1)}, ...), condition=%wide.region_16.17_spmd, body=%wide.region_15.16_spmd.sunk | while | flops 283926 | bytes 7880035 | solution.py:30
  450.2 2.7 constant_dynamic-slice_fusion.5
  453.0 2.0 copy.254
  454.9 3.2 bitcast_add_fusion.11
  458.9 2.7 constant_dynamic-slice_fusion.5
  461.6 2.0 copy.254
  463.6 3.2 bitcast_add_fusion.11
  467.6 2.7 constant_dynamic-slice_fusion.5
  470.3 2.0 copy.254
  472.3 3.2 bitcast_add_fusion.11
  476.2 2.7 constant_dynamic-slice_fusion.5
  479.0 2.0 copy.254
  480.9 3.2 bitcast_add_fusion.11
  484.9 2.7 constant_dynamic-slice_fusion.5
  487.6 2.0 copy.254
  489.6 3.2 bitcast_add_fusion.11
  493.6 2.7 constant_dynamic-slice_fusion.5
  496.3 2.0 copy.254
  498.2 3.2 bitcast_add_fusion.11
  502.2 2.7 constant_dynamic-slice_fusion.5
  504.9 2.0 copy.254
  506.9 3.2 bitcast_add_fusion.11
  510.9 5.5 %fusion.10 = f32[16,64,128]{2,1,0:T(8,128)} fusion(f32[16,273,64]{2,1,0:T(8,128)} %get-tuple-element.123, f32[128,16,256]{0,2,1:T(8,128)} %bitcast.316, f32[128,16,16]{0,2,1:T(8,128)} %copy-done.17, f32[273]{0:T(512)S(1)} %pad.27.clone), kind=kOutput, calls=%fused_computation.29 | convolution fusion | flops 215814144 | bytes 3871812 | tf_op jit(solution)/shard_map/shf,hfd->shd/dot_general | solution.py:89
  516.4 1.5 add_bitcast_fusion
  518.3 1.1 multiply_reduce_fusion.1
  520.9 3.6 convolution_add_fusion.1
  524.5 2.1 copy.213
  526.5 2.0 fusion.53
  (222 shorter events, 28.0 us)
Async XLA Ops:
  7.2 185.4 %all-gather.7.cloned.1.call-start = ((), (), s32[]{:S(2)}) async-start(), calls=%async_computation | async-start | bytes 14155776 | tf_op jit(solution)/shard_map/all_gather | solution.py:21
  8.2 41.1 %copy-start.24 = (bf16[128,256]{0,1:T(8,128)(2,1)}, bf16[128,256]{0,1:T(8,128)(2,1)S(1)}, u32[]{:S(2)}) copy-start(bf16[128,256]{0,1:T(8,128)(2,1)S(1)} %copy.149) | copy-start | bytes 196612
  8.2 4.3 copy-start.17
  9.4 2.7 copy-start.13
  9.7 2.8 copy-start.2
  9.7 2.5 copy-start.26
  9.7 2.6 copy-start.51
  12.1 436.6 %all-gather.9.cloned.1.call-start = ((), (), s32[]{:S(2)}) async-start(), calls=%async_computation.1 | async-start | bytes 14155776 | tf_op jit(solution)/shard_map/all_gather | solution.py:21
  12.3 184.4 %copy-start.18 = (f32[128,1024]{0,1:T(8,128)}, f32[128,1024]{0,1:T(8,128)S(1)}, u32[]{:S(2)}) copy-start(f32[128,1024]{0,1:T(8,128)S(1)} %copy.176) | copy-start | bytes 1572868
  12.5 38.2 %copy-start.22 = (bf16[128,256]{0,1:T(8,128)(2,1)}, bf16[128,256]{0,1:T(8,128)(2,1)S(1)}, u32[]{:S(2)}) copy-start(bf16[128,256]{0,1:T(8,128)(2,1)S(1)} %copy.152) | copy-start | bytes 196612
  49.2 3.1 copy-start.53
  49.2 1.4 copy-start.7
  49.3 147.5 %copy-start.28 = (f32[128,16,16]{0,2,1:T(8,128)}, f32[128,16,16]{0,2,1:T(8,128)S(1)}, u32[]{:S(2)}) copy-start(f32[128,16,16]{0,2,1:T(8,128)S(1)} %broadcast_multiply_fusion) | copy-start | bytes 393220
  194.1 2.7 copy-start.3
  196.8 2.9 copy-start.16
  196.8 2.9 copy-start.27
  199.7 11.6 %copy-start.50 = (bf16[128,1024]{1,0:T(8,128)(2,1)S(1)}, bf16[128,1024]{1,0:T(8,128)(2,1)}, u32[]{:S(2)}) copy-start(bf16[128,1024]{1,0:T(8,128)(2,1)} %param.12) | copy-start | bytes 786436
  199.8 21.9 %collective-permute-start = (bf16[2,128,1024]{2,1,0:T(8,128)(2,1)S(1)}, bf16[2,128,1024]{2,1,0:T(8,128)(2,1)S(1)}, u32[]{:S(2)}, u32[]{:S(2)}) collective-permute-start(bf16[2,128,1024]{2,1,0:T(8,128)(2,1)S(1)} %pad_maximum_fusion.6), channel_id=1, source_target_pairs={{0,1},{1,2},{2,3},{3,4},{4,5},{5,6},{6,7},{8,9},{9,10},{10,11},{11... | collective-permute-start | bytes 1572872 | tf_op jit(solution)/shard_map/ppermute | solution.py:36
  211.4 12.3 %copy-start.46 = (bf16[128,256]{0,1:T(8,128)(2,1)}, bf16[128,256]{0,1:T(8,128)(2,1)S(1)}, u32[]{:S(2)}) copy-start(bf16[128,256]{0,1:T(8,128)(2,1)S(1)} %copy.169) | copy-start | bytes 196612
  213.3 18.5 %copy-start.43 = (bf16[128,256]{0,1:T(8,128)(2,1)}, bf16[128,256]{0,1:T(8,128)(2,1)S(1)}, u32[]{:S(2)}) copy-start(bf16[128,256]{0,1:T(8,128)(2,1)S(1)} %copy.157) | copy-start | bytes 196612
  222.5 3.0 copy-start.40
  223.2 2.3 copy-start.48
  223.7 3.1 copy-start.56
  223.7 4.0 copy-start.45
  225.4 2.1 copy-start.41
  225.9 2.3 copy-start.57
  225.9 2.5 copy-start.36
  227.6 4.6 copy-start.37
  227.7 4.6 copy-start.30
  228.2 4.1 copy-start.33
  231.8 3.7 copy-start.32
  232.3 5.6 %copy-start.35 = (f32[4,128,256]{1,2,0:T(8,128)}, f32[4,128,256]{1,2,0:T(8,128)S(1)}, u32[]{:S(2)}) copy-start(f32[4,128,256]{1,2,0:T(8,128)S(1)} %get-tuple-element.236) | copy-start | bytes 1572868
  232.3 4.2 copy-start.58
  232.3 4.2 copy-start.59
  232.4 4.1 copy-start.42
  238.0 2.2 copy-start.47
  239.1 1.4 copy-start.49
  239.5 1.5 copy-start.34
  239.5 1.5 copy-start.38
  240.6 1.9 copy-start.39
  240.9 2.8 copy-start.44
  244.3 3.9 copy-start.9
  244.3 3.7 copy-start.31
  244.4 1.0 copy-start.11
  245.4 24.2 %copy-start.1 = (f32[16,273,64]{2,1,0:T(8,128)S(1)}, f32[16,273,64]{2,1,0:T(8,128)}, u32[]{:S(2)}) copy-start(f32[16,273,64]{2,1,0:T(8,128)} %get-tuple-element.121) | copy-start | bytes 3354628
  246.3 22.1 %collective-permute-start.1 = (bf16[2,128,1024]{2,1,0:T(8,128)(2,1)}, bf16[2,128,1024]{2,1,0:T(8,128)(2,1)}, u32[]{:S(2)}, u32[]{:S(2)}) collective-permute-start(bf16[2,128,1024]{2,1,0:T(8,128)(2,1)} %pad_maximum_fusion.7), channel_id=1, source_target_pairs={{1,0},{2,1},{3,2},{4,3},{5,4},{6,5},{7,6},{9,8},{10,9},{11,10},{12... | collective-permute-start | bytes 1572872 | tf_op jit(solution)/shard_map/ppermute | solution.py:36
  269.7 4.1 copy-start.14
  269.7 4.1 copy-start.19
  269.7 4.1 copy-start.54
  269.7 4.1 copy-start.60
  277.3 2.2 copy-start.20
  277.3 4.3 copy-start.52
  279.4 4.2 copy-start.5
  282.5 1.1 copy-start.25
  282.5 2.2 copy-start.4
  283.6 95.0 %copy-start.29 = (f32[128,256]{1,0:T(8,128)S(1)}, f32[128,256]{1,0:T(8,128)}, u32[]{:S(2)}) copy-start(f32[128,256]{1,0:T(8,128)} %copy.174) | copy-start | bytes 393220
  284.8 93.9 %copy-start.21 = (f32[128,1024]{1,0:T(8,128)S(1)}, f32[128,1024]{1,0:T(8,128)}, u32[]{:S(2)}) copy-start(f32[128,1024]{1,0:T(8,128)} %copy.175) | copy-start | bytes 1572868
  510.9 5.5 %copy-start = (f32[16,273,64]{2,1,0:T(8,128)S(1)}, f32[16,273,64]{2,1,0:T(8,128)}, u32[]{:S(2)}) copy-start(f32[16,273,64]{2,1,0:T(8,128)} %get-tuple-element.123) | copy-start | bytes 3354628
  510.9 5.5 %copy-start.15 = (bf16[128,1024]{0,1:T(8,128)(2,1)S(1)}, bf16[128,1024]{0,1:T(8,128)(2,1)}, u32[]{:S(2)}) copy-start(bf16[128,1024]{0,1:T(8,128)(2,1)} %copy-done.13) | copy-start | bytes 786436
  518.2 1.2 copy-start.6
  518.2 1.2 copy-start.23
  518.3 2.6 copy-start.55
  520.9 5.7 %copy-start.10 = (f32[256,1024]{1,0:T(8,128)S(1)}, f32[256,1024]{1,0:T(8,128)}, u32[]{:S(2)}) copy-start(f32[256,1024]{1,0:T(8,128)} %copy-done.9) | copy-start | bytes 3145732
  520.9 5.7 %copy-start.12 = (f32[256,1024]{1,0:T(8,128)S(1)}, f32[256,1024]{1,0:T(8,128)}, u32[]{:S(2)}) copy-start(f32[256,1024]{1,0:T(8,128)} %copy-done.11) | copy-start | bytes 3145732
  (1 other events, 0.9 us)
Sparse Core Ops, SparseCore 0:
  12.2 180.3 all-gather.6
  199.8 248.8 all-gather.8
where the time goes:
time: 537 us; the launch traced here: 535 us
  waiting for transfers between devices  234 us (44%)
  blocking collectives  127 us (24%)
  local copies, waits for them, and re-layouts  57 us (11%)
  matrix products  45.6 us (8%)
  other arithmetic  43.1 us (8%)
  between operations  15.3 us (3%)
  starting transfers between devices  13 us (2%)
    all_gather x2, waiting for transfers between devices, carried_in(): gathered = jax.tree.map(lambda a: lax.all_gather(a, axis), part)  209 us
    all_gather x2, blocking collectives, carried_in(): gathered = jax.tree.map(lambda a: lax.all_gather(a, axis), part)  127 us
    dynamic_slice x14, local copies, waits for them, and re-layouts, one(): lax.dynamic_index_in_dim(a, source, 0, False)  32.8 us
    add x14, other arithmetic, add_pair(): return (earlier[0] + later[0], earlier[1] + later[1])  27.8 us
    ppermute x2, waiting for transfers between devices, passed_along(): lax.ppermute(value, axis, [(source, source + steps) for source in range(l...  25.4 us
    ppermute x2, starting transfers between devices, passed_along(): lax.ppermute(value, axis, [(source, source + steps) for source in range(l...  13 us
  transfers between devices with their start and end apart: 4, of which 4 were waited for; matrix products, arithmetic and copies ran while one was open for 10% of the time, Pallas kernels for 0%

commit v1 on v0

v1 whole, which is shorter than its diff:
```python
import functools

import jax
import jax.numpy as jnp
from jax import lax
from jax.experimental import pallas as pl
from jax.experimental.pallas import tpu as pltpu
from jax.sharding import PartitionSpec as P

FD = 16
DH = 64
NF = 160
F32 = jnp.float32
BF = jnp.bfloat16


def dot(a, b, ca, cb):
    return lax.dot_general(a, b, (((ca,), (cb,)), ((), ())), preferred_element_type=F32)


def turned(x, d):
    return x if d == 0 else jnp.concatenate([x[d:], x[:d]], 0)


def features(x, query):
    pair = 1.0 / 16.0 if query else 1.0
    parts = [x * x * (pair * 0.5 if query else 1.0)]
    scaled = x * pair
    for d in range(1, 8):
        parts.append(scaled * turned(x, d))
    parts.append(scaled[:8] * x[8:])
    parts.append(x * 0.25 if query else x)
    row = lax.broadcasted_iota(jnp.int32, (8, x.shape[1]), 0)
    parts.append(jnp.where(row == 0, 1.0, 0.0).astype(F32))
    return jnp.concatenate(parts, 0)


def pull(x, d_feat, query):
    pair = 1.0 / 16.0 if query else 1.0
    total = d_feat[0:16] * x * (pair if query else 2.0)
    cross = jnp.zeros_like(x)
    for d in range(1, 8):
        part = d_feat[16 * d : 16 * d + 16]
        cross = cross + part * turned(x, d) + turned(part * x, 16 - d)
    last = d_feat[128:136]
    cross = cross + jnp.concatenate([last * x[8:], last * x[:8]], 0)
    line = d_feat[136:152]
    return total + cross * pair + line * (0.25 if query else 1.0)


def kernel(n, axis, ql, kl, qw, kw, v, g, mixed, gql, gkl, gqw, gkw, gv,
           qt, kt, qf, kf, kern, nown, nall, ncol, s_own, f_in, f_out,
           sb_own, b_in, b_out, rden, dn, win, dwk, dwv, dden, stat_t, stat_in,
           nbown, nball, nbcol, kprev, vprev, qnext, gnext, dqt, dkt,
           halo_s, halo_r, n_s, n_r, nb_s, nb_r, f_s, f_r, b_s, b_r, st_s, st_r):
    me = lax.axis_index(axis)
    tok = ql.shape[0]
    pairs = v.shape[1] // 128
    heads = 2 * pairs
    first, last = me == 0, me == n - 1
    lane = lax.broadcasted_iota(jnp.int32, (1, 128), 1)
    half = [(lane < DH).astype(F32).astype(BF), (lane >= DH).astype(F32).astype(BF)]
    rows = lax.broadcasted_iota(jnp.int32, (tok, tok), 0)
    cols = lax.broadcasted_iota(jnp.int32, (tok, tok), 1)
    lanes2 = lax.broadcasted_iota(jnp.int32, (tok, 128), 1)
    causal = cols <= rows

    def cut(p):
        return pl.ds(pl.multiple_of(p * 128, 128), 128)

    def frow(h):
        return pl.ds(pl.multiple_of(h * FD, FD), FD)

    def remote(src, dst, ss, rs, to):
        return pltpu.make_async_remote_copy(
            src_ref=src, dst_ref=dst, send_sem=ss, recv_sem=rs,
            device_id={axis: to}, device_id_type=pl.DeviceIdType.MESH)

    def halo(which, p):
        src = (kw, v, qw, g)[which]
        dst = (kprev, vprev, qnext, gnext)[which]
        to = me + 1 if which < 2 else me - 1
        return remote(src.at[:, cut(p)], dst.at[:, cut(p)],
                      halo_s.at[which, p], halo_r.at[which, p], to)

    def f_copy(p):
        return remote(f_out.at[p], f_in.at[p], f_s.at[p], f_r.at[p], me + 1)

    def b_copy(p):
        return remote(b_out.at[p], b_in.at[p], b_s.at[p], b_r.at[p], me - 1)

    def n_copy(to):
        return remote(nown, nall.at[me], n_s.at[to], n_r.at[me], to)

    def nb_copy(to):
        return remote(nbown, nball.at[me], nb_s.at[to], nb_r.at[me], to)

    def n_from(j):
        return remote(nown, nall.at[j], n_s.at[j], n_r.at[j], j)

    def nb_from(j):
        return remote(nbown, nball.at[j], nb_s.at[j], nb_r.at[j], j)

    def stats_copy():
        return remote(stat_t, stat_in, st_s, st_r, me - 1)

    def loop(low, high, body):
        def one(i, c):
            body(i)
            return c
        lax.fori_loop(low, high, one, 0)

    barrier = pltpu.get_barrier_semaphore()
    for d in range(1, n):
        pl.semaphore_signal(barrier, inc=1, device_id={axis: lax.rem(me + d, n)},
                            device_id_type=pl.DeviceIdType.MESH)

    qt[...] = ql[...].astype(F32).T
    kt[...] = kl[...].astype(F32).T
    nown[...] = jnp.zeros_like(nown)
    nbown[...] = jnp.zeros_like(nbown)
    dden[...] = jnp.zeros_like(dden)
    ones8 = jnp.ones((8, tok), BF)

    def phase_a(p):
        got = []
        for hh in range(2):
            h = 2 * p + hh
            kfeat = features(kt[frow(h), :], False).astype(BF)
            kf[h] = kfeat
            qf[h] = features(qt[frow(h), :], True).astype(BF)
            nown[pl.ds(h, 1), 0:NF] = dot(ones8, kfeat, 1, 1)[0:1]
            got.append(dot(kfeat, v[:, cut(p)], 1, 0))
        s_own[p] = jnp.where(lane < DH, got[0], got[1])

    loop(0, pairs, phase_a)
    pl.semaphore_wait(barrier, n - 1)
    loop(me + 1, n, lambda j: n_copy(j).start())

    def send_halo(p):
        @pl.when(jnp.logical_not(last))
        def _():
            halo(0, p).start()
            halo(1, p).start()

        @pl.when(jnp.logical_not(first))
        def _():
            halo(2, p).start()
            halo(3, p).start()

    @pl.when(first)
    def _():
        kprev[...] = jnp.zeros_like(kprev)
        vprev[...] = jnp.zeros_like(vprev)
        f_in[...] = jnp.zeros_like(f_in)

    @pl.when(last)
    def _():
        qnext[...] = jnp.zeros_like(qnext)
        gnext[...] = jnp.zeros_like(gnext)
        stat_in[...] = jnp.zeros_like(stat_in)
        b_in[...] = jnp.zeros_like(b_in)

    def gathered(low, high, arrive, slots):
        def one(j, total):
            arrive(j).wait_recv()
            return total + slots[j]
        total = lax.fori_loop(low, high, one, jnp.zeros(nown.shape, F32))
        full = jnp.concatenate([total, jnp.zeros((128 - heads, nown.shape[1]), F32)], 0)
        return full.T[0:NF].astype(BF)

    loop(0, pairs, send_halo)
    ncol[...] = gathered(0, me, n_from, nall)

    def lin_scores(h):
        return dot(qt[frow(h), :].astype(BF), kt[frow(h), :].astype(BF), 0, 0) * 0.25

    def phase_c(p):
        inv = []
        for hh in range(2):
            h = 2 * p + hh
            s = lin_scores(h)
            kk = jnp.where(causal, 1.0 + s + 0.5 * s * s, 0.0)
            kern[h] = kk.astype(BF)
            prior = dot(qf[h], ncol[...], 0, 0)
            den = jnp.sum(kk + jnp.where(lanes2 == h, prior, 0.0), 1, keepdims=True)
            inv.append(1.0 / den)
        r = jnp.where(lane < DH, inv[0], inv[1])
        rden[p] = r
        low = (g[:, cut(p)].astype(F32) * r).astype(BF)
        dn[:, cut(p)] = low
        sb_own[p] = jnp.where(lane < DH, dot(qf[2 * p], low, 1, 0), dot(qf[2 * p + 1], low, 1, 0))

    loop(0, pairs, phase_c)

    def window(p):
        @pl.when(jnp.logical_not(first))
        def _():
            halo(0, p).wait_recv()
            halo(1, p).wait_recv()
        c = cut(p)
        q, k, vv, gg, kp, vp = qw[:, c], kw[:, c], v[:, c], g[:, c], kprev[:, c], vprev[:, c]
        prior = jnp.logical_and(cols > rows, me > 0)
        keep = []
        for hh in range(2):
            h = 2 * p + hh
            qm, gm = q * half[hh], gg * half[hh]
            so = jnp.where(causal, dot(qm, k, 1, 1) * 0.125, -1e30)
            sp = jnp.where(prior, dot(qm, kp, 1, 1) * 0.125, -1e30)
            m = jnp.max(jnp.maximum(so, sp), 1, keepdims=True)
            eo, ep = jnp.exp(so - m), jnp.exp(sp - m)
            total = jnp.sum(eo + ep, 1, keepdims=True)
            inv = 1.0 / total
            ao, ap = eo * inv, ep * inv
            lo, lp = ao.astype(BF), ap.astype(BF)
            res = dot(lo, vv, 1, 0) + dot(lp, vp, 1, 0)
            inner = jnp.sum(gm.astype(F32) * res, 1, keepdims=True)
            do = (ao * (dot(gm, vv, 1, 1) - inner)).astype(BF)
            dp = (ap * (dot(gm, vp, 1, 1) - inner)).astype(BF)
            dq = dot(do, k, 1, 0) + dot(dp, kp, 1, 0)
            keep.append((res, dq, dot(do, q, 0, 0), dot(lo, gg, 0, 0)))
            logsum = m + jnp.log(total)
            dden[...] += jnp.where(lanes2 == h, logsum, 0.0) + jnp.where(lanes2 == heads + h, inner, 0.0)
        res, dq, dk, dv = [jnp.where(lane < DH, a, b) for a, b in zip(*keep)]
        win[:, c] = res
        gqw[:, c] = (dq * 0.125).astype(BF)
        dwk[:, c] = dk
        dwv[:, c] = dv

    def f_step(p):
        @pl.when(jnp.logical_not(first))
        def _():
            f_copy(p).wait_recv()

        @pl.when(jnp.logical_not(last))
        def _():
            f_out[p] = (f_in[p].astype(F32) + s_own[p]).astype(BF)
            f_copy(p).start()

    def b_step(p):
        @pl.when(jnp.logical_not(last))
        def _():
            b_copy(p).wait_recv()

        @pl.when(jnp.logical_not(first))
        def _():
            b_out[p] = (b_in[p].astype(F32) + sb_own[p]).astype(BF)
            b_copy(p).start()

    def wave(j):
        fp = j - me

        @pl.when(jnp.logical_and(fp >= 0, fp < pairs))
        def _():
            f_step(fp)
        bp = j - (n - 1 - me)

        @pl.when(jnp.logical_and(bp >= 0, bp < pairs))
        def _():
            b_step(bp)

        @pl.when(j < pairs)
        def _():
            window(j)

    loop(0, pairs + n - 1, wave)
    stat_t[...] = dden[...].T[0 : 2 * heads]
    dden[...] = jnp.zeros_like(dden)

    @pl.when(jnp.logical_not(first))
    def _():
        stats_copy().start()

    def phase_d(p):
        c = cut(p)
        vv, low, r, pre = v[:, c], dn[:, c], rden[p], f_in[p]
        num = [dot(kern[2 * p + hh], vv, 1, 0) + dot(qf[2 * p + hh], pre, 0, 0) for hh in range(2)]
        out = jnp.where(lane < DH, num[0], num[1]) * r
        mixed[:, c] = (out + win[:, c]).astype(BF)
        prod = g[:, c].astype(F32) * out * r
        both = jnp.concatenate([pre, ncol[...]], 1)
        for hh in range(2):
            h = 2 * p + hh
            dd = -jnp.sum(jnp.where((lane < DH) == (hh == 0), prod, 0.0), 1, keepdims=True)
            spread = jnp.where(lanes2 == h, dd, 0.0)
            dden[...] += spread
            dm = low * half[hh]
            ds = jnp.where(causal, dot(dm, vv, 1, 1) + dd, 0.0) * (1.0 + lin_scores(h))
            ds = ds.astype(BF)
            d_feat = dot(both, jnp.concatenate([dm, spread.astype(BF)], 1), 1, 1)
            x = qt[frow(h), :]
            dqt[frow(h), :] = dot(kt[frow(h), :].astype(BF), ds, 1, 1) * 0.25 + pull(x, d_feat, True)
            dkt[frow(h), :] = dot(x.astype(BF), ds, 1, 0) * 0.25

    loop(0, pairs, phase_d)
    gql[...] = dqt[...].T.astype(BF)
    dden[...] = dden[...].T

    def back_norm(h):
        one = jnp.broadcast_to(dden[pl.ds(h, 1), :], (8, tok)).astype(BF)
        nbown[pl.ds(h, 1), 0:NF] = dot(one, qf[h], 1, 1)[0:1]

    loop(0, heads, back_norm)
    loop(0, me, lambda j: nb_copy(j).start())

    @pl.when(jnp.logical_not(last))
    def _():
        stats_copy().wait_recv()

    def key_side(p):
        @pl.when(jnp.logical_not(last))
        def _():
            halo(2, p).wait_recv()
            halo(3, p).wait_recv()
        c = cut(p)
        k, vv, q, gg = kw[:, c], v[:, c], qnext[:, c], gnext[:, c]
        live = jnp.logical_and(rows > cols, me < n - 1)
        keep = []
        for hh in range(2):
            h = 2 * p + hh
            s = dot(k * half[hh], q, 1, 1) * 0.125
            a = jnp.exp(jnp.where(live, s - stat_in[pl.ds(h, 1), :], -1e30))
            ds = a * (dot(vv * half[hh], gg, 1, 1) - stat_in[pl.ds(heads + h, 1), :])
            keep.append((dot(ds.astype(BF), q, 1, 0), dot(a.astype(BF), gg, 1, 0)))
        dk, dv = [jnp.where(lane < DH, a, b) for a, b in zip(*keep)]
        gkw[:, c] = ((dwk[:, c] + dk) * 0.125).astype(BF)
        dwv[:, c] += dv

    loop(0, pairs, key_side)
    nbcol[...] = gathered(me + 1, n, nb_from, nball)

    def phase_e(p):
        c = cut(p)
        vv, low, post = v[:, c], dn[:, c], b_in[p]
        both = jnp.concatenate([post, nbcol[...]], 1)
        got = []
        for hh in range(2):
            h = 2 * p + hh
            got.append(dot(kern[h], low, 0, 0) + dot(kf[h], post, 0, 0))
            pick = jnp.where(lanes2 == h, 1.0, 0.0).astype(BF)
            d_feat = dot(both, jnp.concatenate([vv * half[hh], pick], 1), 1, 1)
            dkt[frow(h), :] += pull(kt[frow(h), :], d_feat, False)
        gv[:, c] = (jnp.where(lane < DH, got[0], got[1]) + dwv[:, c]).astype(BF)

    loop(0, pairs, phase_e)
    gkl[...] = dkt[...].T.astype(BF)

    def drain(p):
        @pl.when(jnp.logical_not(last))
        def _():
            halo(0, p).wait_send()
            halo(1, p).wait_send()
            f_copy(p).wait_send()

        @pl.when(jnp.logical_not(first))
        def _():
            halo(2, p).wait_send()
            halo(3, p).wait_send()
            b_copy(p).wait_send()

    loop(0, pairs, drain)
    loop(me + 1, n, lambda j: n_copy(j).wait_send())
    loop(0, me, lambda j: nb_copy(j).wait_send())

    @pl.when(jnp.logical_not(first))
    def _():
        stats_copy().wait_send()


def local(n, axis, *args):
    ql, v = args[0], args[4]
    tok, width = v.shape
    lin = ql.shape[1]
    pairs = width // 128
    heads = 2 * pairs
    vm = pltpu.VMEM
    dma = pltpu.SemaphoreType.DMA
    state16 = vm((pairs, NF, 128), BF)
    state32 = vm((pairs, NF, 128), F32)
    rows = vm((heads, 256), F32)
    wide32 = vm((tok, width), F32)
    wide16 = vm((tok, width), BF)
    lin32 = vm((lin, tok), F32)
    scratch = [
        lin32, lin32, vm((heads, NF, tok), BF), vm((heads, NF, tok), BF), vm((heads, tok, tok), BF),
        rows, vm((n, heads, 256), F32), vm((NF, 128), BF), state32, state16, state16,
        state32, state16, state16, vm((pairs, tok, 128), F32), wide16, wide32, wide32, wide32,
        vm((tok, 128), F32), vm((2 * heads, tok), F32), vm((2 * heads, tok), F32),
        rows, vm((n, heads, 256), F32), vm((NF, 128), BF),
        wide16, wide16, wide16, wide16, lin32, lin32,
        dma((4, pairs)), dma((4, pairs)), dma((n,)), dma((n,)), dma((n,)), dma((n,)),
        dma((pairs,)), dma((pairs,)), dma((pairs,)), dma((pairs,)), dma, dma,
    ]
    order = (v, ql, ql, v, v, v)
    whole = pl.BlockSpec(memory_space=pltpu.VMEM)
    return pl.pallas_call(
        functools.partial(kernel, n, axis),
        out_shape=tuple(jax.ShapeDtypeStruct(a.shape, BF) for a in order),
        in_specs=[whole] * 6,
        out_specs=tuple([whole] * 6),
        scratch_shapes=scratch,
        compiler_params=pltpu.CompilerParams(
            collective_id=0, has_side_effects=True, vmem_limit_bytes=40 * 1024 * 1024),
    )(*args)


def solution(mesh):
    place = P(("dp", "seq"), None)
    return jax.shard_map(
        functools.partial(local, mesh.shape["seq"], "seq"),
        mesh=mesh,
        in_specs=(place,) * 6,
        out_specs=(place,) * 6,
        check_vma=False,
    )
```

time: 537 us -> 100 us (0.19)
  waiting for transfers between devices: 234 us -> 0 us
  blocking collectives: 127 us -> 0 us
  Pallas kernels: 0 us -> 89.5 us
  local copies, waits for them, and re-layouts: 57 us -> 9.54 us
  matrix products: 45.6 us -> 0 us
  other arithmetic: 43.1 us -> 0 us
  between operations: 15.3 us -> 0.66 us
  starting transfers between devices: 13 us -> 0 us
    all_gather x2 -> x0, waiting for transfers between devices: 209 us -> none  [carried_in(): gathered = jax.tree.map(lambda a: lax.all_gather(a, axis), part)]
    all_gather x2 -> x0, blocking collectives: 127 us -> none  [carried_in(): gathered = jax.tree.map(lambda a: lax.all_gather(a, axis), part)]
    pallas_call x0 -> x1, Pallas kernels: none -> 89.5 us  [local(): pl.pallas_call(functools.partial(kernel, n, axis), out_shape=tuple((jax.S...]
    dot_general x34 -> x0, matrix products: 44 us -> none  [the longest x1 5.53 us: linear_grads(): jnp.einsum('shf,hfd->shd', key_feat, next_state, precision=HIGH)]
    dynamic_slice x14 -> x0, local copies, waits for them, and re-layouts: 32.8 us -> none  [one(): lax.dynamic_index_in_dim(a, source, 0, False)]
    add x17 -> x0, other arithmetic: 27.8 us -> none  [the longest x14 27.8 us: add_pair(): return (earlier[0] + later[0], earlier[1] + later[1])]
    ppermute x2 -> x0, waiting for transfers between devices: 25.4 us -> none  [passed_along(): lax.ppermute(value, axis, [(source, source + steps) for source in range(l...]
    ppermute x2 -> x0, starting transfers between devices: 13 us -> none  [passed_along(): lax.ppermute(value, axis, [(source, source + steps) for source in range(l...]
  transfers between devices with their start and end apart: 4 -> 0, of which waited for: 4 -> 0; matrix products, arithmetic and copies ran while one was open for 10% -> 0% of each run, Pallas kernels for 0% -> 0%
where the time goes in v1:
time: 100 us; the launch traced here: 99.7 us
  Pallas kernels  89.5 us (90%)
  local copies, waits for them, and re-layouts  9.54 us (10%)
    pallas_call x1, Pallas kernels, local(): pl.pallas_call(functools.partial(kernel, n, axis), out_shape=tuple((jax.S...  89.5 us
    unnamed x18, local copies, waits for them, and re-layouts  9.54 us

profile of v1, /device:TPU:0, one launch (start us, length us, event | category | flops | bytes accessed | tf_op | source)
XLA Modules:
  0.0 99.7 jit_solution(2489678908754995759)
XLA Ops:
  0.6 0.0 copy-start
  0.6 0.9 copy-done
  1.6 0.0 copy-start.1
  1.6 0.9 copy-done.1
  2.5 0.0 copy-start.2
  2.5 0.9 copy-done.2
  3.5 0.0 copy-start.3
  3.5 0.9 copy-done.3
  4.4 0.0 copy-start.4
  4.4 0.8 copy-done.4
  5.3 0.0 copy-start.5
  5.3 0.8 copy-done.5
  6.1 89.5 %shard_map.109 = (bf16[128,1024]{1,0:T(8,128)(2,1)S(1)}, bf16[128,256]{1,0:T(8,128)(2,1)S(1)}, bf16[128,256]{1,0:T(8,128)(2,1)S(1)}, bf16[128,1024]{1,0:T(8,128)...) custom-call(bf16[128,256]{1,0:T(8,128)(2,1)S(1)} %copy-done.4, bf16[128,256]{1,0:T(8,128)(2,1)S(1)} %copy-done.5, ...), custom_call_target="tpu_custom_call" | custom-call | tf_op jit(solution)/shard_map/pallas_call | solution.py:396
  95.6 0.7 copy.18
  96.3 0.6 copy.19
  96.9 0.6 copy.20
  97.6 0.7 copy.21
  98.3 0.7 copy.22
  99.0 0.7 copy.23
Async XLA Ops:
  0.6 1.0 copy-start
  1.6 0.9 copy-start.1
  2.5 0.9 copy-start.2
  3.5 0.9 copy-start.3
  4.4 0.8 copy-start.4
  5.3 0.8 copy-start.5

commit v2 on v1

v2 whole, which is shorter than its diff:
```python
import functools

import jax
import jax.numpy as jnp
from jax import lax
from jax.experimental import pallas as pl
from jax.experimental.pallas import tpu as pltpu
from jax.sharding import PartitionSpec as P

FD = 16
DH = 64
NF = 160
F32 = jnp.float32
BF = jnp.bfloat16


def dot(a, b, ca, cb):
    return lax.dot_general(a, b, (((ca,), (cb,)), ((), ())), preferred_element_type=F32)


def turned(x, d):
    return x if d == 0 else jnp.concatenate([x[d:], x[:d]], 0)


def features(x, query):
    pair = 1.0 / 16.0 if query else 1.0
    parts = [x * x * (pair * 0.5 if query else 1.0)]
    scaled = x * pair
    for d in range(1, 8):
        parts.append(scaled * turned(x, d))
    parts.append(scaled[:8] * x[8:])
    parts.append(x * 0.25 if query else x)
    row = lax.broadcasted_iota(jnp.int32, (8, x.shape[1]), 0)
    parts.append(jnp.where(row == 0, 1.0, 0.0).astype(F32))
    return jnp.concatenate(parts, 0)


def pull(x, d_feat, query):
    pair = 1.0 / 16.0 if query else 1.0
    total = d_feat[0:16] * x * (pair if query else 2.0)
    cross = jnp.zeros_like(x)
    for d in range(1, 8):
        part = d_feat[16 * d : 16 * d + 16]
        cross = cross + part * turned(x, d) + turned(part * x, 16 - d)
    last = d_feat[128:136]
    cross = cross + jnp.concatenate([last * x[8:], last * x[:8]], 0)
    line = d_feat[136:152]
    return total + cross * pair + line * (0.25 if query else 1.0)


def kernel(n, axis, ql_h, kl_h, qw_h, kw_h, v_h, g_h, mixed, gql, gkl, gqw, gkw, gv,
           ql, kl, qw, kw, v, g,
           qt, kt, qf, kf, kern, plus, ksum, nown, nall, ncol, s_own, f_in, f_out,
           sb_own, b_in, b_out, rden, dn, win, dwk, dwv, dden, stat, stat_t, stat_in,
           nbown, nball, nbcol, kprev, vprev, qnext, gnext, dqt, dkt,
           in_s, halo_s, halo_r, n_s, n_r, nb_s, nb_r, f_s, f_r, b_s, b_r, st_s, st_r):
    me = lax.axis_index(axis)
    tok = ql.shape[0]
    pairs = v.shape[1] // 128
    heads = 2 * pairs
    first, last = me == 0, me == n - 1
    lane = lax.broadcasted_iota(jnp.int32, (1, 128), 1)
    half = [(lane < DH).astype(F32).astype(BF), (lane >= DH).astype(F32).astype(BF)]
    rows = lax.broadcasted_iota(jnp.int32, (tok, tok), 0)
    cols = lax.broadcasted_iota(jnp.int32, (tok, tok), 1)
    lanes2 = lax.broadcasted_iota(jnp.int32, (tok, 128), 1)
    causal = cols <= rows
    causal2 = jnp.concatenate([causal, causal], 0)

    def cut(p):
        return pl.ds(pl.multiple_of(p * 128, 128), 128)

    def prow(p):
        return pl.ds(pl.multiple_of(p * 2 * FD, 2 * FD), 2 * FD)

    def both_halves(x):
        return jnp.concatenate([x * half[0], x * half[1]], 0)

    def pick(x):
        m = x.shape[0] // 2
        return jnp.where(lane < DH, x[:m], x[m:])

    def remote(src, dst, ss, rs, to):
        return pltpu.make_async_remote_copy(
            src_ref=src, dst_ref=dst, send_sem=ss, recv_sem=rs,
            device_id={axis: to}, device_id_type=pl.DeviceIdType.MESH)

    def halo(which, p):
        src = (kw_h, v_h, qw_h, g_h)[which]
        dst = (kprev, vprev, qnext, gnext)[which]
        to = me + 1 if which < 2 else me - 1
        return remote(src.at[:, cut(p)], dst.at[:, cut(p)],
                      halo_s.at[which, p], halo_r.at[which, p], to)

    def f_copy(p):
        return remote(f_out.at[p], f_in.at[p], f_s.at[p], f_r.at[p], me + 1)

    def b_copy(p):
        return remote(b_out.at[p], b_in.at[p], b_s.at[p], b_r.at[p], me - 1)

    def n_copy(to):
        return remote(nown, nall.at[me], n_s.at[to], n_r.at[me], to)

    def nb_copy(to):
        return remote(nbown, nball.at[me], nb_s.at[to], nb_r.at[me], to)

    def n_from(j):
        return remote(nown, nall.at[j], n_s.at[j], n_r.at[j], j)

    def nb_from(j):
        return remote(nbown, nball.at[j], nb_s.at[j], nb_r.at[j], j)

    def stats_copy():
        return remote(stat_t, stat_in, st_s, st_r, me - 1)

    def loop(low, high, body):
        def one(i, c):
            body(i)
            return c
        lax.fori_loop(low, high, one, 0)

    barrier = pltpu.get_barrier_semaphore()
    for d in range(1, n):
        pl.semaphore_signal(barrier, inc=1, device_id={axis: lax.rem(me + d, n)},
                            device_id_type=pl.DeviceIdType.MESH)

    fetch = [pltpu.make_async_copy(a, b, in_s.at[i]) for i, (a, b) in enumerate(
        ((kl_h, kl), (v_h, v), (ql_h, ql), (g_h, g), (kw_h, kw), (qw_h, qw)))]
    for f in fetch:
        f.start()
    nown[...] = jnp.zeros_like(nown)
    nbown[...] = jnp.zeros_like(nbown)
    dden[...] = jnp.zeros_like(dden)
    stat[...] = jnp.zeros_like(stat)
    ones8 = jnp.ones((8, tok), BF)

    @pl.when(first)
    def _():
        kprev[...] = jnp.zeros_like(kprev)
        vprev[...] = jnp.zeros_like(vprev)
        f_in[...] = jnp.zeros_like(f_in)

    @pl.when(last)
    def _():
        qnext[...] = jnp.zeros_like(qnext)
        gnext[...] = jnp.zeros_like(gnext)
        stat_in[...] = jnp.zeros_like(stat_in)
        b_in[...] = jnp.zeros_like(b_in)

    fetch[0].wait()
    kt[...] = kl[...].astype(F32).T
    fetch[1].wait()

    def pair_features(x, query):
        return jnp.concatenate([features(x[:FD], query), features(x[FD:], query)], 0).astype(BF)

    def phase_a(p):
        feats = pair_features(kt[prow(p), :], False)
        kf[p] = feats
        nown[pl.ds(2 * p, 1), 0:NF] = dot(ones8, feats[:NF], 1, 1)[0:1]
        nown[pl.ds(2 * p + 1, 1), 0:NF] = dot(ones8, feats[NF:], 1, 1)[0:1]
        s_own[p] = pick(dot(feats, v[:, cut(p)], 1, 0))

    loop(0, pairs, phase_a)
    pl.semaphore_wait(barrier, n - 1)
    loop(me + 1, n, lambda j: n_copy(j).start())

    def send_front(p):
        @pl.when(jnp.logical_not(last))
        def _():
            halo(0, p).start()
            halo(1, p).start()

    def send_back(p):
        @pl.when(jnp.logical_not(first))
        def _():
            halo(2, p).start()
            halo(3, p).start()

    loop(0, pairs, send_front)
    fetch[2].wait()
    qt[...] = ql[...].astype(F32).T

    def spread_q(p):
        x = qt[prow(p), :].astype(BF)
        z = jnp.zeros((FD, tok), BF)
        return jnp.concatenate(
            [jnp.concatenate([x[:FD], z], 0), jnp.concatenate([z, x[FD:]], 0)], 1)

    def phase_b(p):
        qf[p] = pair_features(qt[prow(p), :], True)
        s = dot(spread_q(p), kt[prow(p), :].astype(BF), 0, 0) * 0.25
        kk = jnp.where(causal2, 1.0 + s + 0.5 * s * s, 0.0)
        kern[p] = kk.astype(BF)
        plus[p] = 1.0 + s
        ksum[p] = pick(jnp.broadcast_to(jnp.sum(kk, 1, keepdims=True), (2 * tok, 128)))

    loop(0, pairs, phase_b)

    def gathered(low, high, arrive, slots):
        def one(j, total):
            arrive(j).wait_recv()
            return total + slots[j]
        total = lax.fori_loop(low, high, one, jnp.zeros(nown.shape, F32))
        full = jnp.concatenate([total, jnp.zeros((128 - heads, nown.shape[1]), F32)], 0)
        return full.T[0:NF].astype(BF)

    ncol[...] = gathered(0, me, n_from, nall)
    fetch[3].wait()

    def phase_c(p):
        prior = []
        for hh in range(2):
            every = dot(qf[p, hh * NF : (hh + 1) * NF], ncol[...], 0, 0)
            prior.append(jnp.sum(jnp.where(lanes2 == 2 * p + hh, every, 0.0), 1, keepdims=True))
        r = 1.0 / (ksum[p] + jnp.where(lane < DH, prior[0], prior[1]))
        rden[p] = r
        low = (g[:, cut(p)].astype(F32) * r).astype(BF)
        dn[:, cut(p)] = low
        sb_own[p] = pick(dot(qf[p], low, 1, 0))

    loop(0, pairs, phase_c)
    fetch[4].wait()
    fetch[5].wait()

    def window(p):
        @pl.when(jnp.logical_not(first))
        def _():
            halo(0, p).wait_recv()
            halo(1, p).wait_recv()
        c = cut(p)
        k = jnp.concatenate([kw[:, c], kprev[:, c]], 0)
        vv = jnp.concatenate([v[:, c], vprev[:, c]], 0)
        qs, gs = both_halves(qw[:, c]), both_halves(g[:, c])
        prior = jnp.logical_and(cols > rows, me > 0)
        seen = jnp.concatenate([causal, prior], 1)
        seen = jnp.concatenate([seen, seen], 0)
        s = jnp.where(seen, dot(qs, k, 1, 1) * 0.125, -1e30)
        m = jnp.max(s, 1, keepdims=True)
        e = jnp.exp(s - m)
        total = jnp.sum(e, 1, keepdims=True)
        a = e * (1.0 / total)
        low = a.astype(BF)
        res = dot(low, vv, 1, 0)
        inner = jnp.sum(gs.astype(F32) * res, 1, keepdims=True)
        ds = (a * (dot(gs, vv, 1, 1) - inner)).astype(BF)
        win[:, c] = pick(res)
        gqw[:, c] = (pick(dot(ds, k, 1, 0)) * 0.125).astype(BF)
        dwk[:, c] = dot(ds[:, :tok], qs, 0, 0)
        dwv[:, c] = dot(low[:, :tok], gs, 0, 0)
        logsum = m + jnp.log(total)
        old = stat[...]
        for hh in range(2):
            part = slice(hh * tok, (hh + 1) * tok)
            old = jnp.where(lanes2 == 2 * p + hh, logsum[part], old)
            old = jnp.where(lanes2 == heads + 2 * p + hh, inner[part], old)
        stat[...] = old

    def f_step(p):
        @pl.when(jnp.logical_not(first))
        def _():
            f_copy(p).wait_recv()

        @pl.when(jnp.logical_not(last))
        def _():
            f_out[p] = (f_in[p].astype(F32) + s_own[p]).astype(BF)
            f_copy(p).start()

    def b_step(p):
        @pl.when(jnp.logical_not(last))
        def _():
            b_copy(p).wait_recv()

        @pl.when(jnp.logical_not(first))
        def _():
            b_out[p] = (b_in[p].astype(F32) + sb_own[p]).astype(BF)
            b_copy(p).start()

    def phase_d(p):
        c = cut(p)
        vv, r, pre = v[:, c], rden[p], f_in[p]
        num = dot(kern[p], vv, 1, 0)
        num = jnp.where(lane < DH, num[:tok] + dot(qf[p, :NF], pre, 0, 0),
                        num[tok:] + dot(qf[p, NF:], pre, 0, 0))
        out = num * r
        mixed[:, c] = (out + win[:, c]).astype(BF)
        prod = g[:, c].astype(F32) * out * r
        zero = jnp.zeros_like(prod)
        dd = -jnp.sum(jnp.concatenate(
            [jnp.where(lane < DH, prod, zero), jnp.where(lane < DH, zero, prod)], 0), 1, keepdims=True)
        one_head = [jnp.where(lanes2 == 2 * p + hh, dd[hh * tok : (hh + 1) * tok], 0.0) for hh in range(2)]
        dden[...] += one_head[0] + one_head[1]
        dm = both_halves(dn[:, c])
        ds = jnp.where(causal2, dot(dm, vv, 1, 1) + dd, 0.0) * plus[p]
        ds = ds.astype(BF)
        d_feat = dot(jnp.concatenate([pre, ncol[...]], 1),
                     jnp.concatenate([dm, jnp.concatenate(one_head, 0).astype(BF)], 1), 1, 1)
        x = qt[prow(p), :]
        dq = dot(kt[prow(p), :].astype(BF), ds, 1, 1) * 0.25
        dqt[prow(p), :] = jnp.concatenate(
            [dq[:FD, :tok] + pull(x[:FD], d_feat[:, :tok], True),
             dq[FD:, tok:] + pull(x[FD:], d_feat[:, tok:], True)], 0)
        dkt[prow(p), :] = dot(spread_q(p), ds, 1, 0) * 0.25

    def wave(j):
        fp = j - me

        @pl.when(jnp.logical_and(fp >= 0, fp < pairs))
        def _():
            f_step(fp)
        bp = j - (n - 1 - me)

        @pl.when(jnp.logical_and(bp >= 0, bp < pairs))
        def _():
            b_step(bp)

        @pl.when(j < pairs)
        def _():
            send_back(j)
            window(j)

        @pl.when(j == pairs - 1)
        def _():
            stat_t[...] = stat[...].T[0 : 2 * heads]

            @pl.when(jnp.logical_not(first))
            def _():
                stats_copy().start()

        @pl.when(j >= n - 1)
        def _():
            phase_d(j - (n - 1))

    loop(0, pairs + n - 1, wave)
    dden[...] = dden[...].T

    def back_norm(h):
        one = jnp.broadcast_to(dden[pl.ds(h, 1), :], (8, tok)).astype(BF)
        feats = qf[h // 2, pl.ds(pl.multiple_of(lax.rem(h, 2) * NF, 16), NF), :]
        nbown[pl.ds(h, 1), 0:NF] = dot(one, feats, 1, 1)[0:1]

    loop(0, heads, back_norm)
    loop(0, me, lambda j: nb_copy(j).start())
    gql[...] = dqt[...].T.astype(BF)

    @pl.when(jnp.logical_not(last))
    def _():
        stats_copy().wait_recv()

    def key_side(p):
        @pl.when(jnp.logical_not(last))
        def _():
            halo(2, p).wait_recv()
            halo(3, p).wait_recv()
        c = cut(p)
        q, gg = qnext[:, c], gnext[:, c]
        live = jnp.logical_and(rows > cols, me < n - 1)
        s = dot(both_halves(kw[:, c]), q, 1, 1) * 0.125
        da = dot(both_halves(v[:, c]), gg, 1, 1)
        aa, dd = [], []
        for hh in range(2):
            part = slice(hh * tok, (hh + 1) * tok)
            h = 2 * p + hh
            a = jnp.exp(jnp.where(live, s[part] - stat_in[pl.ds(h, 1), :], -1e30))
            aa.append(a.astype(BF))
            dd.append((a * (da[part] - stat_in[pl.ds(heads + h, 1), :])).astype(BF))
        dk = dot(jnp.concatenate(dd, 1), both_halves(q), 1, 0)
        gkw[:, c] = ((dwk[:, c] + dk) * 0.125).astype(BF)
        dwv[:, c] += dot(jnp.concatenate(aa, 1), both_halves(gg), 1, 0)

    loop(0, pairs, key_side)
    nbcol[...] = gathered(me + 1, n, nb_from, nball)

    def phase_e(p):
        c = cut(p)
        vv, post = v[:, c], b_in[p]
        dv = dot(kern[p], both_halves(dn[:, c]), 0, 0) + dot(kf[p], both_halves(post), 0, 0)
        gv[:, c] = (dv + dwv[:, c]).astype(BF)
        one_head = [jnp.where(lanes2 == 2 * p + hh, 1.0, 0.0).astype(BF) for hh in range(2)]
        d_feat = dot(jnp.concatenate([post, nbcol[...]], 1),
                     jnp.concatenate([both_halves(vv), jnp.concatenate(one_head, 0)], 1), 1, 1)
        x = kt[prow(p), :]
        dkt[prow(p), :] += jnp.concatenate(
            [pull(x[:FD], d_feat[:, :tok], False), pull(x[FD:], d_feat[:, tok:], False)], 0)

    loop(0, pairs, phase_e)
    gkl[...] = dkt[...].T.astype(BF)

    def drain(p):
        @pl.when(jnp.logical_not(last))
        def _():
            halo(0, p).wait_send()
            halo(1, p).wait_send()
            f_copy(p).wait_send()

        @pl.when(jnp.logical_not(first))
        def _():
            halo(2, p).wait_send()
            halo(3, p).wait_send()
            b_copy(p).wait_send()

    loop(0, pairs, drain)
    loop(me + 1, n, lambda j: n_copy(j).wait_send())
    loop(0, me, lambda j: nb_copy(j).wait_send())

    @pl.when(jnp.logical_not(first))
    def _():
        stats_copy().wait_send()


def writer(*refs):
    count = 6
    held, load_s, store_s = refs[2 * count : 3 * count], refs[-2], refs[-1]
    loads = [pltpu.make_async_copy(refs[i], held[i], load_s.at[i]) for i in range(count)]
    stores = [pltpu.make_async_copy(held[i], refs[count + i], store_s.at[i]) for i in range(count)]
    for c in loads:
        c.start()
    for c, d in zip(loads, stores):
        c.wait()
        d.start()
    for d in stores:
        d.wait()


def local(n, axis, *args):
    ql, v = args[0], args[4]
    tok, width = v.shape
    lin = ql.shape[1]
    pairs = width // 128
    heads = 2 * pairs
    vm = pltpu.VMEM
    dma = pltpu.SemaphoreType.DMA
    state16 = vm((pairs, NF, 128), BF)
    state32 = vm((pairs, NF, 128), F32)
    rows = vm((heads, 256), F32)
    wide32 = vm((tok, width), F32)
    wide16 = vm((tok, width), BF)
    lin16 = vm((tok, lin), BF)
    lin32 = vm((lin, tok), F32)
    tile32 = vm((pairs, tok, 128), F32)
    feats = vm((pairs, 2 * NF, tok), BF)
    small = vm((tok, 128), F32)
    scratch = [
        lin16, lin16, wide16, wide16, wide16, wide16,
        lin32, lin32, feats, feats, vm((pairs, 2 * tok, tok), BF), vm((pairs, 2 * tok, tok), F32), tile32,
        rows, vm((n, heads, 256), F32), vm((NF, 128), BF), state32, state16, state16,
        state32, state16, state16, tile32, wide16, wide32, wide32, wide32,
        small, small, vm((2 * heads, tok), F32), vm((2 * heads, tok), F32),
        rows, vm((n, heads, 256), F32), vm((NF, 128), BF),
        wide16, wide16, wide16, wide16, lin32, lin32,
        dma((6,)), dma((4, pairs)), dma((4, pairs)), dma((n,)), dma((n,)), dma((n,)), dma((n,)),
        dma((pairs,)), dma((pairs,)), dma((pairs,)), dma((pairs,)), dma, dma,
    ]
    order = (v, ql, ql, v, v, v)
    shapes = tuple(jax.ShapeDtypeStruct(a.shape, BF) for a in order)
    hbm = pl.BlockSpec(memory_space=pltpu.HBM)
    anywhere = pl.BlockSpec(memory_space=pl.ANY)
    made = pl.pallas_call(
        functools.partial(kernel, n, axis),
        out_shape=shapes,
        in_specs=[hbm] * 6,
        out_specs=tuple([pl.BlockSpec(memory_space=pltpu.VMEM)] * 6),
        scratch_shapes=scratch,
        compiler_params=pltpu.CompilerParams(
            collective_id=0, has_side_effects=True, vmem_limit_bytes=60 * 1024 * 1024),
    )(*args)
    return pl.pallas_call(
        writer,
        out_shape=shapes,
        in_specs=[anywhere] * 6,
        out_specs=tuple([anywhere] * 6),
        scratch_shapes=[vm(a.shape, BF) for a in order] + [dma((6,)), dma((6,))],
        compiler_params=pltpu.CompilerParams(vmem_limit_bytes=60 * 1024 * 1024),
    )(*made)


def solution(mesh):
    place = P(("dp", "seq"), None)
    return jax.shard_map(
        functools.partial(local, mesh.shape["seq"], "seq"),
        mesh=mesh,
        in_specs=(place,) * 6,
        out_specs=(place,) * 6,
        check_vma=False,
    )
```

time: 100 us -> 80.9 us (0.81)
  local copies, waits for them, and re-layouts: 9.54 us -> 0 us
  Pallas kernels: 89.5 us -> 80.1 us
    unnamed x18 -> x0, local copies, waits for them, and re-layouts: 9.54 us -> none
    pallas_call x1 -> x2, Pallas kernels: 89.5 us -> 80.1 us  [the longest x1 78 us: local(): pl.pallas_call(functools.partial(kernel, n, axis), out_shape=shapes, in_s...]
where the time goes in v2:
time: 80.9 us; the launch traced here: 80.7 us
  Pallas kernels  80.1 us (99%)
    pallas_call x1, Pallas kernels, local(): pl.pallas_call(functools.partial(kernel, n, axis), out_shape=shapes, in_s...  78 us
    pallas_call x1, Pallas kernels, local(): pl.pallas_call(writer, out_shape=shapes, in_specs=[anywhere] * 6, out_spe...  2.07 us

profile of v2, /device:TPU:0, one launch (start us, length us, event | category | flops | bytes accessed | tf_op | source)
XLA Modules:
  0.0 80.7 jit_solution(7969958861168784017)
XLA Ops:
  0.6 78.0 %shard_map.109 = (bf16[128,1024]{1,0:T(8,128)(2,1)}, bf16[128,256]{1,0:T(8,128)(2,1)}, bf16[128,256]{1,0:T(8,128)(2,1)}, bf16[128,1024]{1,0:T(8,128)(2,1)}, bf16...) custom-call(bf16[128,256]{1,0:T(8,128)(2,1)} %ql_h.1, bf16[128,256]{1,0:T(8,128)(2,1)} %kl_h.1, bf16[128,1024]{1,0:T(8,128)(2,1)} %qw_h.1, ...), custom_call_target="tpu_custom_call" | custom-call | tf_op jit(solution)/shard_map/pallas_call | solution.py:458
  78.6 2.1 %shard_map.110 = (bf16[128,1024]{1,0:T(8,128)(2,1)}, bf16[128,256]{1,0:T(8,128)(2,1)}, bf16[128,256]{1,0:T(8,128)(2,1)}, bf16[128,1024]{1,0:T(8,128)(2,1)}, bf16...) custom-call(bf16[128,1024]{1,0:T(8,128)(2,1)} %get-tuple-element.12.refs_0_, ...), custom_call_target="tpu_custom_call" | custom-call | tf_op jit(solution)/shard_map/pallas_call | solution.py:467

commit v3 on v2

--- a/solution.py
+++ b/solution.py
@@ -147,6 +147,21 @@
         stat_in[...] = jnp.zeros_like(stat_in)
         b_in[...] = jnp.zeros_like(b_in)
 
+    def send_front(p):
+        @pl.when(jnp.logical_not(last))
+        def _():
+            halo(0, p).start()
+            halo(1, p).start()
+
+    def send_back(p):
+        @pl.when(jnp.logical_not(first))
+        def _():
+            halo(2, p).start()
+            halo(3, p).start()
+
+    pl.semaphore_wait(barrier, n - 1)
+    early = 2
+    loop(0, early, send_front)
     fetch[0].wait()
     kt[...] = kl[...].astype(F32).T
     fetch[1].wait()
@@ -162,22 +177,8 @@
         s_own[p] = pick(dot(feats, v[:, cut(p)], 1, 0))
 
     loop(0, pairs, phase_a)
-    pl.semaphore_wait(barrier, n - 1)
     loop(me + 1, n, lambda j: n_copy(j).start())
 
-    def send_front(p):
-        @pl.when(jnp.logical_not(last))
-        def _():
-            halo(0, p).start()
-            halo(1, p).start()
-
-    def send_back(p):
-        @pl.when(jnp.logical_not(first))
-        def _():
-            halo(2, p).start()
-            halo(3, p).start()
-
-    loop(0, pairs, send_front)
     fetch[2].wait()
     qt[...] = ql[...].astype(F32).T
 
@@ -187,7 +188,39 @@
         return jnp.concatenate(
             [jnp.concatenate([x[:FD], z], 0), jnp.concatenate([z, x[FD:]], 0)], 1)
 
+    def f_step(p):
+        @pl.when(jnp.logical_not(first))
+        def _():
+            f_copy(p).wait_recv()
+
+        @pl.when(jnp.logical_not(last))
+        def _():
+            f_out[p] = (f_in[p].astype(F32) + s_own[p]).astype(BF)
+            f_copy(p).start()
+
+    def b_step(p):
+        @pl.when(jnp.logical_not(last))
+        def _():
+            b_copy(p).wait_recv()
+
+        @pl.when(jnp.logical_not(first))
+        def _():
+            b_out[p] = (b_in[p].astype(F32) + sb_own[p]).astype(BF)
+            b_copy(p).start()
+
+    def f_wave(t):
+        p = t - me
+
+        @pl.when(jnp.logical_and(p >= 0, p < pairs))
+        def _():
+            f_step(p)
+
     def phase_b(p):
+        f_wave(p)
+
+        @pl.when(p + early < pairs)
+        def _():
+            send_front(p + early)
         qf[p] = pair_features(qt[prow(p), :], True)
         s = dot(spread_q(p), kt[prow(p), :].astype(BF), 0, 0) * 0.25
         kk = jnp.where(causal2, 1.0 + s + 0.5 * s * s, 0.0)
@@ -209,6 +242,8 @@
     fetch[3].wait()
 
     def phase_c(p):
+        f_wave(pairs + p)
+        send_back(p)
         prior = []
         for hh in range(2):
             every = dot(qf[p, hh * NF : (hh + 1) * NF], ncol[...], 0, 0)
@@ -220,6 +255,7 @@
         sb_own[p] = pick(dot(qf[p], low, 1, 0))
 
     loop(0, pairs, phase_c)
+    loop(2 * pairs, pairs + n - 1, f_wave)
     fetch[4].wait()
     fetch[5].wait()
 
@@ -256,26 +292,6 @@
             old = jnp.where(lanes2 == heads + 2 * p + hh, inner[part], old)
         stat[...] = old
 
-    def f_step(p):
-        @pl.when(jnp.logical_not(first))
-        def _():
-            f_copy(p).wait_recv()
-
-        @pl.when(jnp.logical_not(last))
-        def _():
-            f_out[p] = (f_in[p].astype(F32) + s_own[p]).astype(BF)
-            f_copy(p).start()
-
-    def b_step(p):
-        @pl.when(jnp.logical_not(last))
-        def _():
-            b_copy(p).wait_recv()
-
-        @pl.when(jnp.logical_not(first))
-        def _():
-            b_out[p] = (b_in[p].astype(F32) + sb_own[p]).astype(BF)
-            b_copy(p).start()
-
     def phase_d(p):
         c = cut(p)
         vv, r, pre = v[:, c], rden[p], f_in[p]
@@ -302,51 +318,6 @@
              dq[FD:, tok:] + pull(x[FD:], d_feat[:, tok:], True)], 0)
         dkt[prow(p), :] = dot(spread_q(p), ds, 1, 0) * 0.25
 
-    def wave(j):
-        fp = j - me
-
-        @pl.when(jnp.logical_and(fp >= 0, fp < pairs))
-        def _():
-            f_step(fp)
-        bp = j - (n - 1 - me)
-
-        @pl.when(jnp.logical_and(bp >= 0, bp < pairs))
-        def _():
-            b_step(bp)
-
-        @pl.when(j < pairs)
-        def _():
-            send_back(j)
-            window(j)
-
-        @pl.when(j == pairs - 1)
-        def _():
-            stat_t[...] = stat[...].T[0 : 2 * heads]
-
-            @pl.when(jnp.logical_not(first))
-            def _():
-                stats_copy().start()
-
-        @pl.when(j >= n - 1)
-        def _():
-            phase_d(j - (n - 1))
-
-    loop(0, pairs + n - 1, wave)
-    dden[...] = dden[...].T
-
-    def back_norm(h):
-        one = jnp.broadcast_to(dden[pl.ds(h, 1), :], (8, tok)).astype(BF)
-        feats = qf[h // 2, pl.ds(pl.multiple_of(lax.rem(h, 2) * NF, 16), NF), :]
-        nbown[pl.ds(h, 1), 0:NF] = dot(one, feats, 1, 1)[0:1]
-
-    loop(0, heads, back_norm)
-    loop(0, me, lambda j: nb_copy(j).start())
-    gql[...] = dqt[...].T.astype(BF)
-
-    @pl.when(jnp.logical_not(last))
-    def _():
-        stats_copy().wait_recv()
-
     def key_side(p):
         @pl.when(jnp.logical_not(last))
         def _():
@@ -368,9 +339,6 @@
         gkw[:, c] = ((dwk[:, c] + dk) * 0.125).astype(BF)
         dwv[:, c] += dot(jnp.concatenate(aa, 1), both_halves(gg), 1, 0)
 
-    loop(0, pairs, key_side)
-    nbcol[...] = gathered(me + 1, n, nb_from, nball)
-
     def phase_e(p):
         c = cut(p)
         vv, post = v[:, c], b_in[p]
@@ -383,7 +351,58 @@
         dkt[prow(p), :] += jnp.concatenate(
             [pull(x[:FD], d_feat[:, :tok], False), pull(x[FD:], d_feat[:, tok:], False)], 0)
 
-    loop(0, pairs, phase_e)
+    def back_norm(h):
+        one = jnp.broadcast_to(dden[pl.ds(h, 1), :], (8, tok)).astype(BF)
+        feats = qf[h // 2, pl.ds(pl.multiple_of(lax.rem(h, 2) * NF, 16), NF), :]
+        nbown[pl.ds(h, 1), 0:NF] = dot(one, feats, 1, 1)[0:1]
+
+    turns = pairs + n - 1
+    key_at = pairs
+    e_at = max(pairs, n - 1) + 1
+
+    def wave(j):
+        bp = j - (n - 1 - me)
+
+        @pl.when(jnp.logical_and(bp >= 0, bp < pairs))
+        def _():
+            b_step(bp)
+
+        @pl.when(j < pairs)
+        def _():
+            window(j)
+            phase_d(j)
+
+        @pl.when(j == pairs - 1)
+        def _():
+            stat_t[...] = stat[...].T[0 : 2 * heads]
+
+            @pl.when(jnp.logical_not(first))
+            def _():
+                stats_copy().start()
+            dden[...] = dden[...].T
+            loop(0, heads, back_norm)
+            loop(0, me, lambda i: nb_copy(i).start())
+
+        @pl.when(j == key_at)
+        def _():
+            @pl.when(jnp.logical_not(last))
+            def _():
+                stats_copy().wait_recv()
+
+        @pl.when(jnp.logical_and(j >= key_at, j < key_at + pairs))
+        def _():
+            key_side(j - key_at)
+
+        @pl.when(j == e_at)
+        def _():
+            nbcol[...] = gathered(me + 1, n, nb_from, nball)
+
+        @pl.when(jnp.logical_and(j >= e_at, j < e_at + pairs))
+        def _():
+            phase_e(j - e_at)
+
+    loop(0, max(turns, key_at + pairs, e_at + pairs), wave)
+    gql[...] = dqt[...].T.astype(BF)
     gkl[...] = dkt[...].T.astype(BF)
 
     def drain(p):

time: 80.9 us -> 95.3 us (1.18)
  Pallas kernels: 80.1 us -> 94.5 us
    pallas_call x1, Pallas kernels: 78 us -> 92.5 us  [local(): pl.pallas_call(functools.partial(kernel, n, axis), out_shape=shapes, in_s...]
where the time goes in v3:
time: 95.3 us; the launch traced here: 95.2 us
  Pallas kernels  94.5 us (99%)
    pallas_call x1, Pallas kernels, local(): pl.pallas_call(functools.partial(kernel, n, axis), out_shape=shapes, in_s...  92.5 us
    pallas_call x1, Pallas kernels, local(): pl.pallas_call(writer, out_shape=shapes, in_specs=[anywhere] * 6, out_spe...  2.07 us

profile of v3, /device:TPU:0, one launch (start us, length us, event | category | flops | bytes accessed | tf_op | source)
XLA Modules:
  0.0 95.2 jit_solution(12661719740930797242)
XLA Ops:
  0.6 92.5 %shard_map.109 = (bf16[128,1024]{1,0:T(8,128)(2,1)}, bf16[128,256]{1,0:T(8,128)(2,1)}, bf16[128,256]{1,0:T(8,128)(2,1)}, bf16[128,1024]{1,0:T(8,128)(2,1)}, bf16...) custom-call(bf16[128,256]{1,0:T(8,128)(2,1)} %ql_h.1, bf16[128,256]{1,0:T(8,128)(2,1)} %kl_h.1, bf16[128,1024]{1,0:T(8,128)(2,1)} %qw_h.1, ...), custom_call_target="tpu_custom_call" | custom-call | tf_op jit(solution)/shard_map/pallas_call | solution.py:477
  93.1 2.1 %shard_map.110 = (bf16[128,1024]{1,0:T(8,128)(2,1)}, bf16[128,256]{1,0:T(8,128)(2,1)}, bf16[128,256]{1,0:T(8,128)(2,1)}, bf16[128,1024]{1,0:T(8,128)(2,1)}, bf16...) custom-call(bf16[128,1024]{1,0:T(8,128)(2,1)} %get-tuple-element.12.refs_0_, ...), custom_call_target="tpu_custom_call" | custom-call | tf_op jit(solution)/shard_map/pallas_call | solution.py:486

commit v4 on v2

--- a/solution.py
+++ b/solution.py
@@ -50,7 +50,7 @@
 
 def kernel(n, axis, ql_h, kl_h, qw_h, kw_h, v_h, g_h, mixed, gql, gkl, gqw, gkw, gv,
            ql, kl, qw, kw, v, g,
-           qt, kt, qf, kf, kern, plus, ksum, nown, nall, ncol, s_own, f_in, f_out,
+           bias, later, tri, qt, kt, qf, kf, kern, plus, ksum, nown, nall, ncol, s_own, f_in, f_out,
            sb_own, b_in, b_out, rden, dn, win, dwk, dwv, dden, stat, stat_t, stat_in,
            nbown, nball, nbcol, kprev, vprev, qnext, gnext, dqt, dkt,
            in_s, halo_s, halo_r, n_s, n_r, nb_s, nb_r, f_s, f_r, b_s, b_r, st_s, st_r):
@@ -65,7 +65,6 @@
     cols = lax.broadcasted_iota(jnp.int32, (tok, tok), 1)
     lanes2 = lax.broadcasted_iota(jnp.int32, (tok, 128), 1)
     causal = cols <= rows
-    causal2 = jnp.concatenate([causal, causal], 0)
 
     def cut(p):
         return pl.ds(pl.multiple_of(p * 128, 128), 128)
@@ -73,7 +72,9 @@
     def prow(p):
         return pl.ds(pl.multiple_of(p * 2 * FD, 2 * FD), 2 * FD)
 
-    def both_halves(x):
+    def both_halves(x, scale=None):
+        if scale is not None:
+            x = x * jnp.asarray(scale, BF)
         return jnp.concatenate([x * half[0], x * half[1]], 0)
 
     def pick(x):
@@ -133,6 +134,13 @@
     dden[...] = jnp.zeros_like(dden)
     stat[...] = jnp.zeros_like(stat)
     ones8 = jnp.ones((8, tok), BF)
+    never = jnp.full((tok, tok), -1e30, F32)
+    none = jnp.zeros((tok, tok), F32)
+    tri[...] = jnp.where(causal, 1.0, 0.0)
+    bias[:, :tok] = jnp.where(causal, none, never)
+    bias[:, tok:] = jnp.where(jnp.logical_and(cols > rows, me > 0), none, never)
+    later[...] = jnp.where(jnp.logical_and(rows > cols, me < n - 1), none, never)
+    dkt[...] = jnp.zeros_like(dkt)
 
     @pl.when(first)
     def _():
@@ -182,17 +190,18 @@
     qt[...] = ql[...].astype(F32).T
 
     def spread_q(p):
-        x = qt[prow(p), :].astype(BF)
+        x = (qt[prow(p), :] * 0.25).astype(BF)
         z = jnp.zeros((FD, tok), BF)
         return jnp.concatenate(
             [jnp.concatenate([x[:FD], z], 0), jnp.concatenate([z, x[FD:]], 0)], 1)
 
     def phase_b(p):
         qf[p] = pair_features(qt[prow(p), :], True)
-        s = dot(spread_q(p), kt[prow(p), :].astype(BF), 0, 0) * 0.25
-        kk = jnp.where(causal2, 1.0 + s + 0.5 * s * s, 0.0)
+        s = dot(spread_q(p), kt[prow(p), :].astype(BF), 0, 0)
+        mask = jnp.concatenate([tri[...], tri[...]], 0)
+        kk = mask * (1.0 + s + 0.5 * s * s)
         kern[p] = kk.astype(BF)
-        plus[p] = 1.0 + s
+        plus[p] = mask * (1.0 + s)
         ksum[p] = pick(jnp.broadcast_to(jnp.sum(kk, 1, keepdims=True), (2 * tok, 128)))
 
     loop(0, pairs, phase_b)
@@ -231,11 +240,9 @@
         c = cut(p)
         k = jnp.concatenate([kw[:, c], kprev[:, c]], 0)
         vv = jnp.concatenate([v[:, c], vprev[:, c]], 0)
-        qs, gs = both_halves(qw[:, c]), both_halves(g[:, c])
-        prior = jnp.logical_and(cols > rows, me > 0)
-        seen = jnp.concatenate([causal, prior], 1)
-        seen = jnp.concatenate([seen, seen], 0)
-        s = jnp.where(seen, dot(qs, k, 1, 1) * 0.125, -1e30)
+        qs, gs = both_halves(qw[:, c], 0.125), both_halves(g[:, c])
+        hidden = bias[...]
+        s = dot(qs, k, 1, 1) + jnp.concatenate([hidden, hidden], 0)
         m = jnp.max(s, 1, keepdims=True)
         e = jnp.exp(s - m)
         total = jnp.sum(e, 1, keepdims=True)
@@ -291,7 +298,7 @@
         one_head = [jnp.where(lanes2 == 2 * p + hh, dd[hh * tok : (hh + 1) * tok], 0.0) for hh in range(2)]
         dden[...] += one_head[0] + one_head[1]
         dm = both_halves(dn[:, c])
-        ds = jnp.where(causal2, dot(dm, vv, 1, 1) + dd, 0.0) * plus[p]
+        ds = (dot(dm, vv, 1, 1) + dd) * plus[p]
         ds = ds.astype(BF)
         d_feat = dot(jnp.concatenate([pre, ncol[...]], 1),
                      jnp.concatenate([dm, jnp.concatenate(one_head, 0).astype(BF)], 1), 1, 1)
@@ -300,52 +307,7 @@
         dqt[prow(p), :] = jnp.concatenate(
             [dq[:FD, :tok] + pull(x[:FD], d_feat[:, :tok], True),
              dq[FD:, tok:] + pull(x[FD:], d_feat[:, tok:], True)], 0)
-        dkt[prow(p), :] = dot(spread_q(p), ds, 1, 0) * 0.25
-
-    def wave(j):
-        fp = j - me
-
-        @pl.when(jnp.logical_and(fp >= 0, fp < pairs))
-        def _():
-            f_step(fp)
-        bp = j - (n - 1 - me)
-
-        @pl.when(jnp.logical_and(bp >= 0, bp < pairs))
-        def _():
-            b_step(bp)
-
-        @pl.when(j < pairs)
-        def _():
-            send_back(j)
-            window(j)
-
-        @pl.when(j == pairs - 1)
-        def _():
-            stat_t[...] = stat[...].T[0 : 2 * heads]
-
-            @pl.when(jnp.logical_not(first))
-            def _():
-                stats_copy().start()
-
-        @pl.when(j >= n - 1)
-        def _():
-            phase_d(j - (n - 1))
-
-    loop(0, pairs + n - 1, wave)
-    dden[...] = dden[...].T
-
-    def back_norm(h):
-        one = jnp.broadcast_to(dden[pl.ds(h, 1), :], (8, tok)).astype(BF)
-        feats = qf[h // 2, pl.ds(pl.multiple_of(lax.rem(h, 2) * NF, 16), NF), :]
-        nbown[pl.ds(h, 1), 0:NF] = dot(one, feats, 1, 1)[0:1]
-
-    loop(0, heads, back_norm)
-    loop(0, me, lambda j: nb_copy(j).start())
-    gql[...] = dqt[...].T.astype(BF)
-
-    @pl.when(jnp.logical_not(last))
-    def _():
-        stats_copy().wait_recv()
+        dkt[prow(p), :] += dot(spread_q(p), ds, 1, 0)
 
     def key_side(p):
         @pl.when(jnp.logical_not(last))
@@ -354,36 +316,92 @@
             halo(3, p).wait_recv()
         c = cut(p)
         q, gg = qnext[:, c], gnext[:, c]
-        live = jnp.logical_and(rows > cols, me < n - 1)
-        s = dot(both_halves(kw[:, c]), q, 1, 1) * 0.125
+        q = q * jnp.asarray(0.125, BF)
+        s = dot(both_halves(kw[:, c]), q, 1, 1)
         da = dot(both_halves(v[:, c]), gg, 1, 1)
         aa, dd = [], []
         for hh in range(2):
             part = slice(hh * tok, (hh + 1) * tok)
             h = 2 * p + hh
-            a = jnp.exp(jnp.where(live, s[part] - stat_in[pl.ds(h, 1), :], -1e30))
+            a = jnp.exp(s[part] - stat_in[pl.ds(h, 1), :] + later[...])
             aa.append(a.astype(BF))
             dd.append((a * (da[part] - stat_in[pl.ds(heads + h, 1), :])).astype(BF))
         dk = dot(jnp.concatenate(dd, 1), both_halves(q), 1, 0)
-        gkw[:, c] = ((dwk[:, c] + dk) * 0.125).astype(BF)
+        gkw[:, c] = (dwk[:, c] + dk).astype(BF)
         dwv[:, c] += dot(jnp.concatenate(aa, 1), both_halves(gg), 1, 0)
-
-    loop(0, pairs, key_side)
-    nbcol[...] = gathered(me + 1, n, nb_from, nball)
 
     def phase_e(p):
         c = cut(p)
         vv, post = v[:, c], b_in[p]
         dv = dot(kern[p], both_halves(dn[:, c]), 0, 0) + dot(kf[p], both_halves(post), 0, 0)
-        gv[:, c] = (dv + dwv[:, c]).astype(BF)
-        one_head = [jnp.where(lanes2 == 2 * p + hh, 1.0, 0.0).astype(BF) for hh in range(2)]
-        d_feat = dot(jnp.concatenate([post, nbcol[...]], 1),
-                     jnp.concatenate([both_halves(vv), jnp.concatenate(one_head, 0)], 1), 1, 1)
+        dwv[:, c] += dv
+        pull_keys(p, dot(post, both_halves(vv), 1, 1))
+
+    def pull_keys(p, d_feat):
         x = kt[prow(p), :]
         dkt[prow(p), :] += jnp.concatenate(
             [pull(x[:FD], d_feat[:, :tok], False), pull(x[FD:], d_feat[:, tok:], False)], 0)
 
-    loop(0, pairs, phase_e)
+    def back_norm(h):
+        one = jnp.broadcast_to(dden[pl.ds(h, 1), :], (8, tok)).astype(BF)
+        feats = qf[h // 2, pl.ds(pl.multiple_of(lax.rem(h, 2) * NF, 16), NF), :]
+        nbown[pl.ds(h, 1), 0:NF] = dot(one, feats, 1, 1)[0:1]
+
+    def finish(p):
+        c = cut(p)
+        gv[:, c] = dwv[:, c].astype(BF)
+        one_head = [jnp.where(lanes2 == 2 * p + hh, 1.0, 0.0).astype(BF) for hh in range(2)]
+        pull_keys(p, dot(nbcol[...], jnp.concatenate(one_head, 0), 1, 1))
+
+    hop = 2
+    turns = max(hop * (n - 1), pairs) + pairs
+    key_at = max(pairs + 2, turns - 6)
+    d_at = jnp.maximum(pairs, hop * me)
+    e_at = jnp.maximum(pairs, hop * (n - 1 - me))
+
+    def within(p, body):
+        @pl.when(jnp.logical_and(p >= 0, p < pairs))
+        def _():
+            body(p)
+
+    def wave(j):
+        within(j - hop * me, f_step)
+        within(j - hop * (n - 1 - me), b_step)
+
+        @pl.when(j < pairs)
+        def _():
+            send_back(j)
+            window(j)
+
+        @pl.when(j == pairs - 1)
+        def _():
+            stat_t[...] = stat[...].T[0 : 2 * heads]
+
+            @pl.when(jnp.logical_not(first))
+            def _():
+                stats_copy().start()
+
+        within(j - d_at, phase_d)
+
+        @pl.when(j == d_at + pairs - 1)
+        def _():
+            dden[...] = dden[...].T
+            loop(0, heads, back_norm)
+            loop(0, me, lambda i: nb_copy(i).start())
+
+        within(j - e_at, phase_e)
+
+        @pl.when(jnp.logical_and(j == key_at, jnp.logical_not(last)))
+        def _():
+            stats_copy().wait_recv()
+
+        within(j - key_at, key_side)
+
+    loop(0, turns, wave)
+    loop(min(turns - key_at, pairs), pairs, key_side)
+    gql[...] = dqt[...].T.astype(BF)
+    nbcol[...] = gathered(me + 1, n, nb_from, nball)
+    loop(0, pairs, finish)
     gkl[...] = dkt[...].T.astype(BF)
 
     def drain(p):
@@ -442,6 +460,7 @@
     small = vm((tok, 128), F32)
     scratch = [
         lin16, lin16, wide16, wide16, wide16, wide16,
+        vm((tok, 2 * tok), F32), vm((tok, tok), F32), vm((tok, tok), F32),
         lin32, lin32, feats, feats, vm((pairs, 2 * tok, tok), BF), vm((pairs, 2 * tok, tok), F32), tile32,
         rows, vm((n, heads, 256), F32), vm((NF, 128), BF), state32, state16, state16,
         state32, state16, state16, tile32, wide16, wide32, wide32, wide32,

time: 80.9 us -> 75.9 us (0.938)
  Pallas kernels: 80.1 us -> 75.1 us
    pallas_call x1, Pallas kernels: 78 us -> 73 us  [local(): pl.pallas_call(functools.partial(kernel, n, axis), out_shape=shapes, in_s...]
where the time goes in v4:
time: 75.9 us; the launch traced here: 75.7 us
  Pallas kernels  75.1 us (99%)
    pallas_call x1, Pallas kernels, local(): pl.pallas_call(functools.partial(kernel, n, axis), out_shape=shapes, in_s...  73 us
    pallas_call x1, Pallas kernels, local(): pl.pallas_call(writer, out_shape=shapes, in_specs=[anywhere] * 6, out_spe...  2.07 us

profile of v4, /device:TPU:0, one launch (start us, length us, event | category | flops | bytes accessed | tf_op | source)
XLA Modules:
  0.0 75.7 jit_solution(10937172049748050189)
XLA Ops:
  0.6 73.0 %shard_map.109 = (bf16[128,1024]{1,0:T(8,128)(2,1)}, bf16[128,256]{1,0:T(8,128)(2,1)}, bf16[128,256]{1,0:T(8,128)(2,1)}, bf16[128,1024]{1,0:T(8,128)(2,1)}, bf16...) custom-call(bf16[128,256]{1,0:T(8,128)(2,1)} %ql_h.1, bf16[128,256]{1,0:T(8,128)(2,1)} %kl_h.1, bf16[128,1024]{1,0:T(8,128)(2,1)} %qw_h.1, ...), custom_call_target="tpu_custom_call" | custom-call | tf_op jit(solution)/shard_map/pallas_call | solution.py:477
  73.6 2.1 %shard_map.110 = (bf16[128,1024]{1,0:T(8,128)(2,1)}, bf16[128,256]{1,0:T(8,128)(2,1)}, bf16[128,256]{1,0:T(8,128)(2,1)}, bf16[128,1024]{1,0:T(8,128)(2,1)}, bf16...) custom-call(bf16[128,1024]{1,0:T(8,128)(2,1)} %get-tuple-element.12.refs_0_, ...), custom_call_target="tpu_custom_call" | custom-call | tf_op jit(solution)/shard_map/pallas_call | solution.py:486

commit v5 on v4

--- a/solution.py
+++ b/solution.py
@@ -134,6 +134,8 @@
     dden[...] = jnp.zeros_like(dden)
     stat[...] = jnp.zeros_like(stat)
     ones8 = jnp.ones((8, tok), BF)
+    ones = jnp.ones((128, 128), BF)
+    ones2 = jnp.ones((2 * tok, 128), BF)
     never = jnp.full((tok, tok), -1e30, F32)
     none = jnp.zeros((tok, tok), F32)
     tri[...] = jnp.where(causal, 1.0, 0.0)
@@ -185,7 +187,6 @@
             halo(2, p).start()
             halo(3, p).start()
 
-    loop(0, pairs, send_front)
     fetch[2].wait()
     qt[...] = ql[...].astype(F32).T
 
@@ -196,13 +197,15 @@
             [jnp.concatenate([x[:FD], z], 0), jnp.concatenate([z, x[FD:]], 0)], 1)
 
     def phase_b(p):
+        send_front(p)
         qf[p] = pair_features(qt[prow(p), :], True)
         s = dot(spread_q(p), kt[prow(p), :].astype(BF), 0, 0)
         mask = jnp.concatenate([tri[...], tri[...]], 0)
         kk = mask * (1.0 + s + 0.5 * s * s)
-        kern[p] = kk.astype(BF)
+        low = kk.astype(BF)
+        kern[p] = low
         plus[p] = mask * (1.0 + s)
-        ksum[p] = pick(jnp.broadcast_to(jnp.sum(kk, 1, keepdims=True), (2 * tok, 128)))
+        ksum[p] = pick(dot(low, ones, 1, 0))
 
     loop(0, pairs, phase_b)
 
@@ -245,12 +248,14 @@
         s = dot(qs, k, 1, 1) + jnp.concatenate([hidden, hidden], 0)
         m = jnp.max(s, 1, keepdims=True)
         e = jnp.exp(s - m)
-        total = jnp.sum(e, 1, keepdims=True)
-        a = e * (1.0 / total)
+        res = dot(e.astype(BF), jnp.concatenate([vv, ones2], 1), 1, 0)
+        total = res[:, 128:]
+        inv = 1.0 / total
+        a = e * jnp.concatenate([inv, inv], 1)
         low = a.astype(BF)
-        res = dot(low, vv, 1, 0)
-        inner = jnp.sum(gs.astype(F32) * res, 1, keepdims=True)
-        ds = (a * (dot(gs, vv, 1, 1) - inner)).astype(BF)
+        res = res[:, :128] * inv
+        inner = dot((gs.astype(F32) * res).astype(BF), ones, 1, 0)
+        ds = (a * (dot(gs, vv, 1, 1) - jnp.concatenate([inner, inner], 1))).astype(BF)
         win[:, c] = pick(res)
         gqw[:, c] = (pick(dot(ds, k, 1, 0)) * 0.125).astype(BF)
         dwk[:, c] = dot(ds[:, :tok], qs, 0, 0)
@@ -292,9 +297,7 @@
         out = num * r
         mixed[:, c] = (out + win[:, c]).astype(BF)
         prod = g[:, c].astype(F32) * out * r
-        zero = jnp.zeros_like(prod)
-        dd = -jnp.sum(jnp.concatenate(
-            [jnp.where(lane < DH, prod, zero), jnp.where(lane < DH, zero, prod)], 0), 1, keepdims=True)
+        dd = dot(both_halves(-prod.astype(BF)), ones, 1, 0)
         one_head = [jnp.where(lanes2 == 2 * p + hh, dd[hh * tok : (hh + 1) * tok], 0.0) for hh in range(2)]
         dden[...] += one_head[0] + one_head[1]
         dm = both_halves(dn[:, c])

time: 75.9 us -> 75.8 us (level)
  no operation moved by 1% of the time
where the time goes in v5:
time: 75.8 us; the launch traced here: 75.7 us
  Pallas kernels  75 us (99%)
    pallas_call x1, Pallas kernels, local(): pl.pallas_call(functools.partial(kernel, n, axis), out_shape=shapes, in_s...  73 us
    pallas_call x1, Pallas kernels, local(): pl.pallas_call(writer, out_shape=shapes, in_specs=[anywhere] * 6, out_spe...  2.07 us

profile of v5, /device:TPU:0, one launch (start us, length us, event | category | flops | bytes accessed | tf_op | source)
XLA Modules:
  0.0 75.7 jit_solution(2330865470487335412)
XLA Ops:
  0.6 73.0 %shard_map.109 = (bf16[128,1024]{1,0:T(8,128)(2,1)}, bf16[128,256]{1,0:T(8,128)(2,1)}, bf16[128,256]{1,0:T(8,128)(2,1)}, bf16[128,1024]{1,0:T(8,128)(2,1)}, bf16...) custom-call(bf16[128,256]{1,0:T(8,128)(2,1)} %ql_h.1, bf16[128,256]{1,0:T(8,128)(2,1)} %kl_h.1, bf16[128,1024]{1,0:T(8,128)(2,1)} %qw_h.1, ...), custom_call_target="tpu_custom_call" | custom-call | tf_op jit(solution)/shard_map/pallas_call | solution.py:480
  73.6 2.1 %shard_map.110 = (bf16[128,1024]{1,0:T(8,128)(2,1)}, bf16[128,256]{1,0:T(8,128)(2,1)}, bf16[128,256]{1,0:T(8,128)(2,1)}, bf16[128,1024]{1,0:T(8,128)(2,1)}, bf16...) custom-call(bf16[128,1024]{1,0:T(8,128)(2,1)} %get-tuple-element.12.refs_0_, ...), custom_call_target="tpu_custom_call" | custom-call | tf_op jit(solution)/shard_map/pallas_call | solution.py:489

commit v6 on v5

--- a/solution.py
+++ b/solution.py
@@ -86,11 +86,14 @@
             src_ref=src, dst_ref=dst, send_sem=ss, recv_sem=rs,
             device_id={axis: to}, device_id_type=pl.DeviceIdType.MESH)
 
+    step = tok // pairs
+
     def halo(which, p):
         src = (kw_h, v_h, qw_h, g_h)[which]
         dst = (kprev, vprev, qnext, gnext)[which]
         to = me + 1 if which < 2 else me - 1
-        return remote(src.at[:, cut(p)], dst.at[:, cut(p)],
+        part = pl.ds(pl.multiple_of(p * step, step), step)
+        return remote(src.at[part, :], dst.at[part, :],
                       halo_s.at[which, p], halo_r.at[which, p], to)
 
     def f_copy(p):
@@ -236,10 +239,6 @@
     fetch[5].wait()
 
     def window(p):
-        @pl.when(jnp.logical_not(first))
-        def _():
-            halo(0, p).wait_recv()
-            halo(1, p).wait_recv()
         c = cut(p)
         k = jnp.concatenate([kw[:, c], kprev[:, c]], 0)
         vv = jnp.concatenate([v[:, c], vprev[:, c]], 0)
@@ -313,10 +312,6 @@
         dkt[prow(p), :] += dot(spread_q(p), ds, 1, 0)
 
     def key_side(p):
-        @pl.when(jnp.logical_not(last))
-        def _():
-            halo(2, p).wait_recv()
-            halo(3, p).wait_recv()
         c = cut(p)
         q, gg = qnext[:, c], gnext[:, c]
         q = q * jnp.asarray(0.125, BF)
@@ -367,10 +362,22 @@
         def _():
             body(p)
 
+    def front_here(p):
+        halo(0, p).wait_recv()
+        halo(1, p).wait_recv()
+
+    def back_here(p):
+        halo(2, p).wait_recv()
+        halo(3, p).wait_recv()
+
     def wave(j):
         within(j - hop * me, f_step)
         within(j - hop * (n - 1 - me), b_step)
 
+        @pl.when(jnp.logical_and(j == 0, jnp.logical_not(first)))
+        def _():
+            loop(0, pairs, front_here)
+
         @pl.when(j < pairs)
         def _():
             send_back(j)
@@ -396,6 +403,7 @@
 
         @pl.when(jnp.logical_and(j == key_at, jnp.logical_not(last)))
         def _():
+            loop(0, pairs, back_here)
             stats_copy().wait_recv()
 
         within(j - key_at, key_side)

time: 75.8 us -> 75.6 us (level)
  no operation moved by 1% of the time
where the time goes in v6:
time: 75.6 us; the launch traced here: 75.4 us
  Pallas kernels  74.8 us (99%)
    pallas_call x1, Pallas kernels, local(): pl.pallas_call(functools.partial(kernel, n, axis), out_shape=shapes, in_s...  72.7 us
    pallas_call x1, Pallas kernels, local(): pl.pallas_call(writer, out_shape=shapes, in_specs=[anywhere] * 6, out_spe...  2.07 us

profile of v6, /device:TPU:0, one launch (start us, length us, event | category | flops | bytes accessed | tf_op | source)
XLA Modules:
  0.0 75.4 jit_solution(8094389086756996356)
XLA Ops:
  0.6 72.7 %shard_map.109 = (bf16[128,1024]{1,0:T(8,128)(2,1)}, bf16[128,256]{1,0:T(8,128)(2,1)}, bf16[128,256]{1,0:T(8,128)(2,1)}, bf16[128,1024]{1,0:T(8,128)(2,1)}, bf16...) custom-call(bf16[128,256]{1,0:T(8,128)(2,1)} %ql_h.1, bf16[128,256]{1,0:T(8,128)(2,1)} %kl_h.1, bf16[128,1024]{1,0:T(8,128)(2,1)} %qw_h.1, ...), custom_call_target="tpu_custom_call" | custom-call | tf_op jit(solution)/shard_map/pallas_call | solution.py:488
  73.4 2.1 %shard_map.110 = (bf16[128,1024]{1,0:T(8,128)(2,1)}, bf16[128,256]{1,0:T(8,128)(2,1)}, bf16[128,256]{1,0:T(8,128)(2,1)}, bf16[128,1024]{1,0:T(8,128)(2,1)}, bf16...) custom-call(bf16[128,1024]{1,0:T(8,128)(2,1)} %get-tuple-element.12.refs_0_, ...), custom_call_target="tpu_custom_call" | custom-call | tf_op jit(solution)/shard_map/pallas_call | solution.py:497

commit v7 on v6

--- a/solution.py
+++ b/solution.py
@@ -380,7 +380,6 @@
 
         @pl.when(j < pairs)
         def _():
-            send_back(j)
             window(j)
 
         @pl.when(j == pairs - 1)
@@ -391,6 +390,7 @@
             def _():
                 stats_copy().start()
 
+        within(j - 4, send_back)
         within(j - d_at, phase_d)
 
         @pl.when(j == d_at + pairs - 1)

time: 75.6 us -> 79.7 us (1.054)
  Pallas kernels: 74.8 us -> 78.8 us
    pallas_call x1, Pallas kernels: 72.7 us -> 76.8 us  [local(): pl.pallas_call(functools.partial(kernel, n, axis), out_shape=shapes, in_s...]
where the time goes in v7:
time: 79.7 us; the launch traced here: 79.5 us
  Pallas kernels  78.8 us (99%)
    pallas_call x1, Pallas kernels, local(): pl.pallas_call(functools.partial(kernel, n, axis), out_shape=shapes, in_s...  76.8 us
    pallas_call x1, Pallas kernels, local(): pl.pallas_call(writer, out_shape=shapes, in_specs=[anywhere] * 6, out_spe...  2.07 us

profile of v7, /device:TPU:0, one launch (start us, length us, event | category | flops | bytes accessed | tf_op | source)
XLA Modules:
  0.0 79.5 jit_solution(996120082678249556)
XLA Ops:
  0.6 76.8 %shard_map.109 = (bf16[128,1024]{1,0:T(8,128)(2,1)}, bf16[128,256]{1,0:T(8,128)(2,1)}, bf16[128,256]{1,0:T(8,128)(2,1)}, bf16[128,1024]{1,0:T(8,128)(2,1)}, bf16...) custom-call(bf16[128,256]{1,0:T(8,128)(2,1)} %ql_h.1, bf16[128,256]{1,0:T(8,128)(2,1)} %kl_h.1, bf16[128,1024]{1,0:T(8,128)(2,1)} %qw_h.1, ...), custom_call_target="tpu_custom_call" | custom-call | tf_op jit(solution)/shard_map/pallas_call | solution.py:488
  77.4 2.1 %shard_map.110 = (bf16[128,1024]{1,0:T(8,128)(2,1)}, bf16[128,256]{1,0:T(8,128)(2,1)}, bf16[128,256]{1,0:T(8,128)(2,1)}, bf16[128,1024]{1,0:T(8,128)(2,1)}, bf16...) custom-call(bf16[128,1024]{1,0:T(8,128)(2,1)} %get-tuple-element.12.refs_0_, ...), custom_call_target="tpu_custom_call" | custom-call | tf_op jit(solution)/shard_map/pallas_call | solution.py:497
